TPU v7x, 32 devices: a whole 2x2x4 slice. The times are simulated.
32 devices in a mesh: seq: 32 (over z, y, x, core), mp: 1.
Axes of the slice: x: 2, y: 2, z: 4, core: 2. Of those that a mesh axis runs over, the one named last changes fastest.
Arguments:
- query: bfloat16 [1, 64, 64, 1024], P(None, 'seq', None, 'mp'), may hold values from -6 to 6
- keys: bfloat16 [1, 64, 64, 1024], P(None, 'seq', None, 'mp'), may hold values from -6 to 6
- values: bfloat16 [1, 64, 64, 1024], P(None, 'seq', None, 'mp'), may hold values from -6 to 6
- resid: bfloat16 [1, 64, 64, 1920], P(None, 'seq', 'mp'), may hold values from -4 to 4
- out_weight: bfloat16 [1024, 1920], P('mp'), may hold values from -0.1875 to 0.1875
- norm_gain: float32 [1920], replicated, may hold values from 0.1 to 1.9
- norm_bias: float32 [1920], replicated, may hold values from -3 to 3
- deconv1_weight: bfloat16 [384, 4, 4, 1920], P('mp'), may hold values from -0.0625 to 0.0625
- deconv1_bias: float32 [384], P('mp'), may hold values from -3 to 3
- deconv2_weight: bfloat16 [384, 4, 4, 384], P('mp'), may hold values from -0.15625 to 0.15625
- deconv2_bias: float32 [384], P('mp'), may hold values from -3 to 3
- final_weight: bfloat16 [384, 308], replicated, may hold values from -0.3125 to 0.3125
- final_bias: float32 [308], replicated, may hold values from -3 to 3
Outputs:
- heatmaps: bfloat16 [1, 256, 256, 308], P(None, 'seq', 'mp')
All inputs are finite; a program needn't handle non-finite values.
Results may differ from a plain program's by a relative error of at most 0.012.
Values may be sent and summed in bfloat16 or wider, within the bound.
No kernel may reach another device: no remote copies, remote signals or barrier semaphores. Data moves between devices by JAX's collectives and lax.ppermute only.
A program may use at most 256 MiB of HBM per device.

v0:
```python
import functools

import jax
import jax.numpy as jnp
from jax import lax
from jax.experimental import pallas as pl
from jax.experimental.pallas import tpu as pltpu
from jax.sharding import PartitionSpec as P

HEAD_DIM = 64


TAP_TABLE = (((1, 1), (0, 3)), ((2, 0), (1, 2)))
EPSILON = 1e-06


def with_halo(array, sides, width):
    for axis, dim in sides:
        size, length = (lax.axis_size(axis), array.shape[dim])
        up = [(i, (i + 1) % size) for i in range(size - 1)]
        down = [(j, i) for i, j in up]
        last = lax.slice_in_dim(array, length - width, length, axis=dim)
        first = lax.slice_in_dim(array, 0, width, axis=dim)
        before = lax.ppermute(last, axis, up)
        after = lax.ppermute(first, axis, down)
        array = jnp.concatenate([before, array, after], axis=dim)
    return array


def tap_product(window, weight, kernel_row, kernel_col):
    tap = weight[:, kernel_row, kernel_col, :]
    return lax.dot_general(
        window, tap, (((3,), (1,)), ((), ())), preferred_element_type=jnp.float32
    )


def half_rows(padded, weight, tap_pairs, first_row, row_count):
    col_count = padded.shape[2] - 2
    halves = []
    for col_parity in range(2):
        summed = None
        for pad_row, kernel_row in tap_pairs:
            for pad_col, kernel_col in TAP_TABLE[col_parity]:
                window = padded[
                    :,
                    first_row + pad_row : first_row + pad_row + row_count,
                    pad_col : pad_col + col_count,
                    :,
                ]
                product = tap_product(window, weight, kernel_row, kernel_col)
                summed = product if summed is None else summed + product
        halves.append(summed)
    stacked = jnp.stack(halves, axis=3)
    return stacked.reshape(stacked.shape[0], row_count, 2 * col_count, stacked.shape[-1])


def upsample(padded, weight, row_count):
    even_rows = half_rows(padded, weight, TAP_TABLE[0], 0, row_count)
    odd_rows = half_rows(padded, weight, TAP_TABLE[1], 0, row_count)
    stacked = jnp.stack([even_rows, odd_rows], axis=2)
    return stacked.reshape(stacked.shape[0], 2 * row_count, stacked.shape[3], stacked.shape[4])


def pad_columns(field):
    return jnp.pad(field, ((0, 0), (0, 0), (1, 1), (0, 0)))


def layer_norm(stream, norm_gain, norm_bias):
    center = jnp.mean(stream, axis=-1, keepdims=True)
    shifted = stream - center
    variance = jnp.mean(shifted * shifted, axis=-1, keepdims=True)
    return (shifted * lax.rsqrt(variance + EPSILON) * norm_gain + norm_bias).astype(jnp.bfloat16)


def local(
    query,
    keys,
    values,
    resid,
    out_weight,
    norm_gain,
    norm_bias,
    deconv1_weight,
    deconv1_bias,
    deconv2_weight,
    deconv2_bias,
    final_weight,
    final_bias,
):
    frame_count, row_count, col_count, feature_width = query.shape
    local_heads = feature_width // HEAD_DIM
    score_scale = HEAD_DIM ** (-0.5)
    query_count = row_count * col_count
    queries = query.reshape(frame_count, query_count, local_heads, HEAD_DIM)
    start_max = jnp.full((frame_count, query_count, local_heads), -1e30, jnp.float32)
    running_max = start_max
    key_piece = lax.all_gather(keys, "seq", axis=1, tiled=True).reshape(
        frame_count, -1, local_heads, HEAD_DIM
    )
    value_piece = lax.all_gather(values, "seq", axis=1, tiled=True).reshape(
        frame_count, -1, local_heads, HEAD_DIM
    )
    scores = (
        jnp.einsum("fqhd,fkhd->fqhk", queries, key_piece, preferred_element_type=jnp.float32)
        * score_scale
    )
    fresh_max = jnp.maximum(running_max, jnp.max(scores, axis=-1))
    exps = jnp.exp(scores - fresh_max[..., None])
    denominator = jnp.sum(exps, axis=-1)
    weighted = jnp.einsum(
        "fqhk,fkhd->fqhd",
        exps.astype(jnp.bfloat16),
        value_piece,
        preferred_element_type=jnp.float32,
    )
    running_max, denominator, weighted = (fresh_max, denominator, weighted)
    attended = (
        (weighted / denominator[..., None])
        .astype(jnp.bfloat16)
        .reshape(frame_count, row_count, col_count, feature_width)
    )
    partial_value = jnp.dot(attended, out_weight, preferred_element_type=jnp.float32)
    summed = lax.psum(partial_value.astype(jnp.bfloat16), "mp").astype(jnp.float32)
    full_resid = lax.all_gather(resid, "mp", axis=2, tiled=True)
    normed = layer_norm(full_resid.astype(jnp.float32) + summed, norm_gain, norm_bias)
    rimmed = with_halo(normed, (("seq", 1),), 1)
    padded = pad_columns(rimmed)
    deconv_one = upsample(padded, deconv1_weight, row_count)
    hidden_one = jnp.maximum(deconv_one + deconv1_bias, 0.0).astype(jnp.bfloat16)
    gathered = lax.all_gather(hidden_one, "mp", axis=3, tiled=True)
    middle = with_halo(gathered, (("seq", 1),), 1)
    deconv_two = upsample(pad_columns(middle), deconv2_weight, 2 * row_count)
    hidden_two = jnp.maximum(deconv_two + deconv2_bias, 0.0).astype(jnp.bfloat16)
    return (
        jnp.dot(
            lax.all_to_all(hidden_two, "mp", split_axis=2, concat_axis=3, tiled=True),
            final_weight,
            preferred_element_type=jnp.float32,
        )
        + final_bias
    ).astype(jnp.bfloat16)

LOG2E = 1.4426950408889634
MIB = 1024 * 1024
NT = (((1,), (1,)), ((), ()))


def dot_nt(left, right):
    return lax.dot_general(left, right, NT, preferred_element_type=jnp.float32)


def whole(shape):
    return pl.BlockSpec(shape, lambda *_: (0,) * len(shape))


def pack_kernel(
    query_ref, keys_ref, values_ref, resid_ref, out_ref, first_ref, last_ref, held_ref, done
):
    copies = []
    for index, source in enumerate((query_ref, keys_ref, values_ref)):
        for row in range(2):
            copy = pltpu.make_async_copy(source.at[0, row], held_ref.at[index, row], done.at[2 * index + row])
            copies.append(copy)
    copies.append(pltpu.make_async_copy(resid_ref.at[0, 0], first_ref, done.at[6]))
    copies.append(pltpu.make_async_copy(resid_ref.at[0, 1], last_ref, done.at[7]))
    for copy in copies:
        copy.start()
    for copy in copies[:6]:
        copy.wait()
    for head in range(out_ref.shape[0] // 2):
        lanes = pl.ds(128 * (head // 2), 128)
        own = slice(64 * (head % 2), 64 * (head % 2) + 64)
        for row in range(2):
            block = out_ref.at[2 * head + row]
            queries, keys, values = (held_ref[index, row, :, lanes][:, own] for index in range(3))
            block[0:32, :] = jnp.concatenate([queries[0:32], queries[32:64]], axis=1)
            block[32:96, :] = jnp.concatenate([keys, values], axis=1)
    for copy in copies[6:]:
        copy.wait()


def pack_tokens(query, keys, values, resid, device_count):
    edge = jax.ShapeDtypeStruct(resid.shape[2:], resid.dtype)
    return pl.pallas_call(
        pack_kernel,
        in_specs=[pl.BlockSpec(memory_space=pl.ANY)] * 4,
        out_shape=(jax.ShapeDtypeStruct((device_count, 96, 128), jnp.bfloat16), edge, edge),
        scratch_shapes=[pltpu.VMEM((3,) + query.shape[1:], jnp.bfloat16), pltpu.SemaphoreType.DMA((8,))],
        compiler_params=pltpu.CompilerParams(vmem_limit_bytes=60 * MIB),
        name="pack_tokens",
    )(query, keys, values, resid)


def reorder_kernel(weight_ref, after_ref, out_ref):
    del after_ref
    out_ref[0] = jnp.swapaxes(weight_ref[:, 0], 0, 1)


def reorder_taps(weight, rows, after):
    channels, _, columns, width = weight.shape
    block = channels // 2 if width > 1024 else channels

    def row_at(place):
        row = rows[0]
        for index in range(1, len(rows)):
            row = jnp.where(place == index, rows[index], row)
        return row

    moved = 2 * len(rows) * channels * columns * width * weight.dtype.itemsize
    return pl.pallas_call(
        reorder_kernel,
        grid=(len(rows), channels // block),
        in_specs=[
            pl.BlockSpec((block, 1, columns, width), lambda i, j: (j, row_at(i), 0, 0)),
            pl.BlockSpec(memory_space=pl.ANY),
        ],
        out_specs=pl.BlockSpec((1, columns, block, width), lambda i, j: (i, 0, j, 0)),
        out_shape=jax.ShapeDtypeStruct((len(rows), columns, channels, width), weight.dtype),
        compiler_params=pltpu.CompilerParams(vmem_limit_bytes=60 * MIB),
        cost_estimate=pl.CostEstimate(flops=0, bytes_accessed=moved, transcendentals=0),
        name="reorder_taps",
    )(weight, after)


def attend_kernel(own_ref, other_ref, out_ref, pairs_ref, values_ref, top_ref, total_ref, mixed_ref, *, sources, chunk):
    half = pairs_ref.shape[0] // 2
    count = 2 * half

    @pl.when(pl.program_id(0) == 0)
    def _():
        pairs_ref[0:half, :] = own_ref[:, 32:96, :].reshape(half, 128)
        pairs_ref[half:count, :] = other_ref[...].reshape(half, 128)
        longest = jnp.zeros((1, 1), jnp.float32)
        for start in range(0, count, 512):
            wide = pairs_ref[start : start + 512, :].astype(jnp.float32).T
            values_ref[:, start : start + 512] = wide[64:128].astype(jnp.bfloat16)
            norms = jnp.sum(wide[0:64] * wide[0:64], axis=0, keepdims=True)
            longest = jnp.maximum(longest, jnp.max(norms, axis=1, keepdims=True))
        top_ref[0:1, 0:128] = jnp.broadcast_to(longest, (1, 128))

    first = pl.program_id(0) * sources
    rows = sources * 32
    packed = own_ref[pl.ds(first, sources), 0:32, :].reshape(rows, 128)
    wide = (packed.astype(jnp.float32) * HEAD_DIM ** (-0.5)).T
    zeros = jnp.zeros((64, rows), jnp.float32)
    exact = jnp.concatenate(
        [jnp.concatenate([wide[0:64], wide[64:128]], axis=1), jnp.concatenate([zeros, zeros], axis=1)], axis=0
    )
    queries = exact.astype(jnp.bfloat16)
    norms = jnp.sum(exact * exact, axis=0, keepdims=True)
    bound = 1.01 * jnp.max(norms * top_ref[0:1, 0:1])
    small = bound <= 50.0 * 50.0

    @pl.when(small)
    def _():
        total, mixed = None, None
        for start in range(0, count, chunk):
            scores = jnp.dot(pairs_ref[start : start + chunk, :], queries, preferred_element_type=jnp.float32)
            exps = jnp.exp2(scores * LOG2E)
            part = jnp.sum(exps, axis=0, keepdims=True)
            product = jnp.dot(
                values_ref[:, start : start + chunk], exps.astype(jnp.bfloat16), preferred_element_type=jnp.float32
            )
            total = part if total is None else total + part
            mixed = product if mixed is None else mixed + product
        total_ref[...] = total
        mixed_ref[...] = mixed

    @pl.when(jnp.logical_not(small))
    def _():
        total_ref[...] = jnp.zeros_like(total_ref)
        mixed_ref[...] = jnp.zeros_like(mixed_ref)

        def absorb(index, top):
            start = pl.multiple_of(index * chunk, chunk)
            scores = jnp.dot(pairs_ref[pl.ds(start, chunk), :], queries, preferred_element_type=jnp.float32)
            fresh = jnp.maximum(top, jnp.max(scores, axis=0, keepdims=True))
            exps = jnp.exp2((scores - fresh) * LOG2E)
            shrink = jnp.exp2((top - fresh) * LOG2E)
            product = jnp.dot(
                values_ref[:, pl.ds(start, chunk)], exps.astype(jnp.bfloat16), preferred_element_type=jnp.float32
            )
            total_ref[...] = total_ref[...] * shrink + jnp.sum(exps, axis=0, keepdims=True)
            mixed_ref[...] = mixed_ref[...] * shrink + product
            return fresh

        lax.fori_loop(0, count // chunk, absorb, jnp.full((1, 2 * rows), -1e30, jnp.float32))

    attended = mixed_ref[...] / total_ref[...]
    joined = jnp.concatenate([attended[:, :rows], attended[:, rows:]], axis=0)
    out_ref[...] = joined.T.astype(jnp.bfloat16).reshape(sources, 32, 128)


def attend(own, other, sources=16, chunk=512):
    count = own.shape[0]
    return pl.pallas_call(
        functools.partial(attend_kernel, sources=sources, chunk=chunk),
        grid=(count // sources,),
        in_specs=[whole(own.shape), whole(other.shape)],
        out_specs=pl.BlockSpec((sources, 32, 128), lambda i: (i, 0, 0)),
        out_shape=jax.ShapeDtypeStruct((count, 32, 128), jnp.bfloat16),
        scratch_shapes=[
            pltpu.VMEM((2 * count * 64, 128), jnp.bfloat16),
            pltpu.VMEM((64, 2 * count * 64), jnp.bfloat16),
            pltpu.VMEM((8, 128), jnp.float32),
            pltpu.VMEM((1, 64 * sources), jnp.float32),
            pltpu.VMEM((64, 64 * sources), jnp.float32),
        ],
        compiler_params=pltpu.CompilerParams(vmem_limit_bytes=40 * MIB),
        name="attend",
    )(own, other)


def shift_columns(field, row_length):
    count = field.shape[0]
    column = lax.broadcasted_iota(jnp.int32, field.shape, 0) % row_length
    before = jnp.where(column == 0, 0.0, pltpu.roll(field, 1, 0))
    after = jnp.where(column == row_length - 1, 0.0, pltpu.roll(field, count - 1, 0))
    return before, after


def store_strided(wide_ref, start, value):
    for group in range(wide_ref.shape[0]):
        lanes = slice(128 * group, 128 * group + 128)
        wide_ref[group, pl.ds(start, value.shape[0], stride=2), :] = value[:, lanes]


def load_wide(wide_ref, rows):
    groups = [wide_ref[group, rows, :] for group in range(wide_ref.shape[0])]
    return jnp.concatenate(groups, axis=1).astype(jnp.bfloat16)


def column_taps(parity):
    return ((1, 1), (0, 3)) if parity == 0 else ((1, 2), (2, 0))


def attended_rows(mixed_ref):
    rows = []
    for parity, which in ((1, 0), (0, 0), (1, 1), (0, 1)):
        low, high = [], []
        for head in range(0, mixed_ref.shape[0], 2):
            left, right = mixed_ref[head, parity, which], mixed_ref[head + 1, parity, which]
            low.append(jnp.concatenate([left[:, :64], right[:, :64]], axis=1))
            high.append(jnp.concatenate([left[:, 64:], right[:, 64:]], axis=1))
        rows += [jnp.concatenate(low, axis=1), jnp.concatenate(high, axis=1)]
    return jnp.concatenate(rows, axis=0)


def head_kernel(
    inside_ref,
    mixed_ref,
    resid_ref,
    above_ref,
    below_ref,
    out_weight_ref,
    gain_ref,
    shift_ref,
    first_taps_ref,
    last_taps_ref,
    bias_one_ref,
    taps_two_ref,
    bias_two_ref,
    final_ref,
    final_bias_ref,
    out_ref,
    projection_ref,
    weight_one_ref,
    weight_two_ref,
    field_ref,
    sums_ref,
    wide_one_ref,
    copies_ref,
    wide_two_ref,
    done,
):
    channels = bias_one_ref.shape[1]
    order = ((1, 0), (1, 1), (3, 0), (3, 1), (2, 0), (2, 1), (0, 0), (0, 1))
    slots = weight_one_ref.shape[0]
    ahead = slots - 1
    first = pltpu.make_async_copy(out_weight_ref, projection_ref, done.at[0])
    last = pltpu.make_async_copy(taps_two_ref, weight_two_ref, done.at[1])
    copies = []
    for index, (_, half) in enumerate(order):
        taps = first_taps_ref.at[index // 2] if index < 6 else last_taps_ref.at[0]
        source = taps.at[pl.ds(2 * half, 2)]
        slot = index % slots
        copies.append(pltpu.make_async_copy(source, weight_one_ref.at[slot], done.at[2 + index]))
    first.start()
    copies[0].start()

    attended = attended_rows(mixed_ref)
    first.wait()
    for copy in copies[1:ahead]:
        copy.start()
    projected = jnp.dot(attended, projection_ref[...], preferred_element_type=jnp.float32)
    for place, resid in enumerate((above_ref[...], resid_ref[0], resid_ref[1], below_ref[...])):
        rows = slice(64 * place, 64 * place + 64)
        stream = resid.astype(jnp.float32) + projected[rows]
        center = jnp.mean(stream, axis=-1, keepdims=True)
        shifted = stream - center
        variance = jnp.mean(shifted * shifted, axis=-1, keepdims=True)
        normed = shifted * lax.rsqrt(variance + EPSILON) * gain_ref[...] + shift_ref[...]
        if place in (0, 3):
            normed = jnp.where(inside_ref[place // 3] > 0, normed, 0.0)
        field_ref[rows, :] = normed.astype(jnp.bfloat16)

    for index, (kernel_row, half) in enumerate(order):
        copies[index].wait()
        if index + ahead < len(order):
            copies[index + ahead].start()
        elif index + ahead == len(order):
            last.start()
        low = 64 if kernel_row < 2 else 0
        weight = weight_one_ref[index % slots].reshape(2 * channels, weight_one_ref.shape[3])
        product = dot_nt(field_ref[low : low + 192, :], weight)
        odd, even = product[:, :channels], product[:, channels:]
        if half == 0:
            odd = shift_columns(odd, 64)[1]
        else:
            even = shift_columns(even, 64)[0]
        if index % 4 == 0:
            sums_ref[0] = even
            sums_ref[1] = odd
        else:
            sums_ref[0] += even
            sums_ref[1] += odd
        if index % 4 == 3:
            for parity in range(2):
                hidden = jnp.maximum(sums_ref[parity] + bias_one_ref[...], 0.0)
                for place in range(3):
                    row = 2 * place + (1 if index == 3 else 0)
                    value = hidden[64 * place : 64 * place + 64]
                    if row in (0, 5):
                        value = jnp.where(inside_ref[row // 5] > 0, value, 0.0)
                    store_strided(wide_one_ref, 128 * row + parity, value)

    hidden = load_wide(wide_one_ref, slice(None))
    before, after = shift_columns(hidden.astype(jnp.float32), 128)
    copies_ref[:, 0:channels] = before.astype(jnp.bfloat16)
    copies_ref[:, channels : 2 * channels] = hidden
    copies_ref[:, 2 * channels :] = after.astype(jnp.bfloat16)
    last.wait()
    for row_parity in range(2):
        for parity in range(2):
            total = None
            for low, kernel_row in (((128, 1), (0, 3)), ((128, 2), (256, 0)))[row_parity]:
                for copy, kernel_col in column_taps(parity):
                    product = dot_nt(
                        copies_ref[low : low + 512, copy * channels : (copy + 1) * channels],
                        weight_two_ref[kernel_row, kernel_col],
                    )
                    total = product if total is None else total + product
            hidden = jnp.maximum(total + bias_two_ref[...], 0.0)
            for place in range(4):
                start = 256 * (2 * place + row_parity) + parity
                store_strided(wide_two_ref, start, hidden[128 * place : 128 * place + 128])
    for row in range(8):
        hidden = load_wide(wide_two_ref, slice(256 * row, 256 * row + 256))
        heat = dot_nt(final_ref[...], hidden) + final_bias_ref[...]
        out_ref[row] = heat.astype(jnp.bfloat16)


def keypoint_head(
    inside,
    mixed,
    resid,
    above,
    below,
    out_weight,
    gain,
    shift,
    first_taps,
    last_taps,
    bias_one,
    taps_two,
    bias_two,
    final_weight,
    final_bias,
):
    width = resid.shape[-1]
    channels = bias_one.shape[0]
    keypoints = final_weight.shape[1]
    near = pl.BlockSpec(memory_space=pltpu.VMEM)
    far = pl.BlockSpec(memory_space=pl.ANY)
    return pl.pallas_call(
        head_kernel,
        in_specs=[pl.BlockSpec(memory_space=pltpu.SMEM), near, near, near, near, far, near, near]
        + [far, far, near, far, near, near, near],
        out_shape=jax.ShapeDtypeStruct((8, keypoints, 256), jnp.bfloat16),
        scratch_shapes=[
            pltpu.VMEM(out_weight.shape, jnp.bfloat16),
            pltpu.VMEM((5, 2, channels, width), jnp.bfloat16),
            pltpu.VMEM((4, 4, channels, channels), jnp.bfloat16),
            pltpu.VMEM((256, width), jnp.bfloat16),
            pltpu.VMEM((2, 192, channels), jnp.float32),
            pltpu.VMEM((channels // 128, 768, 128), jnp.float32),
            pltpu.VMEM((768, 3 * channels), jnp.bfloat16),
            pltpu.VMEM((channels // 128, 2048, 128), jnp.float32),
            pltpu.SemaphoreType.DMA((10,)),
        ],
        compiler_params=pltpu.CompilerParams(vmem_limit_bytes=57 * MIB + MIB // 2),
        name="keypoint_head",
    )(
        inside,
        mixed,
        resid,
        above,
        below,
        out_weight,
        gain.reshape(1, -1),
        shift.reshape(1, -1),
        first_taps,
        last_taps,
        bias_one.reshape(1, -1),
        taps_two,
        bias_two.reshape(1, -1),
        final_weight.T,
        final_bias.reshape(-1, 1),
    )


def by_heads(
    query,
    keys,
    values,
    resid,
    out_weight,
    norm_gain,
    norm_bias,
    deconv1_weight,
    deconv1_bias,
    deconv2_weight,
    deconv2_bias,
    final_weight,
    final_bias,
):
    count = lax.axis_size("seq")
    place = lax.axis_index("seq")
    up = [(i, i + 1) for i in range(count - 1)]
    down = [(i + 1, i) for i in range(count - 1)]
    swap = [(i, i ^ 1) for i in range(count)]

    packed, first_row, last_row = pack_tokens(query, keys, values, resid, count)
    own = lax.all_to_all(packed, "seq", 0, 0, tiled=True)
    above = lax.ppermute(last_row, "seq", up)
    below = lax.ppermute(first_row, "seq", down)
    first_taps = reorder_taps(deconv1_weight, (1, 3, 2), packed)
    own, above, below, first_taps = lax.optimization_barrier((own, above, below, first_taps))
    other = lax.ppermute(own[:, 32:96], "seq", swap)
    mixed = attend(own, other)
    last_taps = reorder_taps(deconv1_weight, (0,), mixed)
    taps_two = reorder_taps(deconv2_weight, (0, 1, 2, 3), mixed)

    rim = jnp.zeros((1, 32, 128), jnp.bfloat16)
    earlier = jnp.concatenate([rim, mixed[:-1]], axis=0)
    later = jnp.concatenate([mixed[1:], rim], axis=0)
    odd = place % 2 == 1
    sent = jnp.stack([jnp.where(odd, earlier, mixed), jnp.where(odd, mixed, later)], axis=1)
    back = lax.all_to_all(sent, "seq", 0, 0, tiled=True)
    back = back.reshape(count // 2, 2, 2, 32, 128)

    inside = jnp.stack([place > 0, place < count - 1]).astype(jnp.int32)
    heat = keypoint_head(
        inside,
        back,
        resid[0],
        above,
        below,
        out_weight,
        norm_gain,
        norm_bias,
        first_taps,
        last_taps,
        deconv1_bias,
        taps_two,
        deconv2_bias,
        final_weight,
        final_bias,
    )
    return jnp.transpose(heat, (0, 2, 1))[None]


def step(*arrays):
    query = arrays[0]
    frames, rows, columns, width = query.shape
    heads = width // HEAD_DIM
    whole_heads = lax.axis_size("mp") == 1 and lax.axis_size("seq") == 2 * heads
    if whole_heads and (frames, rows, columns) == (1, 2, 64):
        return by_heads(*arrays)
    return local(*arrays)


def solution(mesh):
    placed = (
        P(None, "seq", None, "mp"),
        P(None, "seq", None, "mp"),
        P(None, "seq", None, "mp"),
        P(None, "seq", "mp", None),
        P("mp", None),
        P(),
        P(),
        P("mp", None, None, None),
        P("mp"),
        P("mp", None, None, None),
        P("mp"),
        P(),
        P(),
    )
    return jax.shard_map(
        step, mesh=mesh, in_specs=placed, out_specs=P(None, "seq", "mp", None), check_vma=False
    )
```

profile of v0, /device:TPU:0, one launch (start us, length us, event | category | flops | bytes accessed | tf_op | source)
XLA Modules:
  0.0 96.8 jit_solution(17341700681991559824)
XLA Ops:
  0.0 2.6 %pack_tokens.1 = (bf16[32,96,128]{2,1,0:T(8,128)(2,1)}, bf16[64,1920]{1,0:T(8,128)(2,1)}, bf16[64,1920]{1,0:T(8,128)(2,1)}) custom-call(bf16[1,2,64,1024]{3,2,1,0:T(8,128)(2,1)} %query_ref.1, bf16[1,2,64,1024]{3,2,1,0:T(8,128)(2,1)} %keys_ref.1, bf16[1,2,64,1024]{3,2,1,0:T(8,128)(2,1)} %values_ref.1, bf16[1,2,64,1920]{3,2,1,0:T(8,128)(2,1)} %resid_ref.1), custom_call_target="tpu_custom_call" | custom-call | tf_op jit(solution)/shard_map/pack_tokens/pallas_call | solution.py:184
  2.6 7.3 %all-to-all-start = ((bf16[32,96,128]{2,1,0:T(8,128)(2,1)}), bf16[32,96,128]{2,1,0:T(8,128)(2,1)S(1)}, u32[]{:S(2)}, u32[]{:S(2)}) async-start(bf16[32,96,128]{2,1,0:T(8,128)(2,1)} %get-tuple-element.12.after_ref), calls=%async_computation | async-start | bytes 1572864 | tf_op jit(solution)/shard_map/all_to_all | solution.py:544
  9.9 2.2 %collective-permute-start = (bf16[64,1920]{1,0:T(8,128)(2,1)}, bf16[64,1920]{1,0:T(8,128)(2,1)S(1)}, u32[]{:S(2)}, u32[]{:S(2)}) collective-permute-start(bf16[64,1920]{1,0:T(8,128)(2,1)} %get-tuple-element.13), channel_id=1, source_target_pairs={{0,1},{1,2},{2,3},{3,4},{4,5},{5,6},{6,7},{7,8},{8,9},{9,10},{10,1... | collective-permute-start | bytes 737288 | tf_op jit(solution)/shard_map/ppermute | solution.py:545
  12.1 1.3 %collective-permute-start.1 = (bf16[64,1920]{1,0:T(8,128)(2,1)}, bf16[64,1920]{1,0:T(8,128)(2,1)S(1)}, u32[]{:S(2)}, u32[]{:S(2)}) collective-permute-start(bf16[64,1920]{1,0:T(8,128)(2,1)} %get-tuple-element.14), channel_id=1, source_target_pairs={{1,0},{2,1},{3,2},{4,3},{5,4},{6,5},{7,6},{8,7},{9,8},{10,9},{11,1... | collective-permute-start | bytes 737288 | tf_op jit(solution)/shard_map/ppermute | solution.py:546
  13.4 14.6 %reorder_taps.3.first_taps_ref = bf16[3,4,384,1920]{3,2,1,0:T(8,128)(2,1)} custom-call(bf16[384,4,4,1920]{3,2,1,0:T(4,128)(2,1)} %weight_ref.4, bf16[32,96,128]{2,1,0:T(8,128)(2,1)} %get-tuple-element.12.after_ref), custom_call_target="tpu_custom_call" | custom-call | bytes 35389440 | tf_op jit(solution)/shard_map/reorder_taps/pallas_call | solution.py:210
  28.0 0.0 copy-start.7
  28.0 0.0 copy-start.8
  28.0 0.0 copy-start.4
  28.0 0.0 copy-start.5
  28.0 0.0 copy-start.6
  28.0 0.0 collective-permute-done.above_ref
  28.0 0.0 copy-start.2
  28.0 0.0 collective-permute-done.1.below_ref
  28.1 0.0 copy-start.3
  28.1 2.4 %all-to-all-done.own_ref = bf16[32,96,128]{2,1,0:T(8,128)(2,1)S(1)} async-done(((bf16[32,96,128]{2,1,0:T(8,128)(2,1)}), bf16[32,96,128]{2,1,0:T(8,128)(2,1)S(1)}, u32[]{:S(2)}, u32[]{:S(2)}) %all-to-all-start) | async-done | bytes 786464 | tf_op jit(solution)/shard_map/all_to_all | solution.py:544
  30.5 0.1 slice.9
  30.6 0.1 collective-permute-start.2
  30.7 1.9 %collective-permute-done.2.other_ref = bf16[32,64,128]{2,1,0:T(8,128)(2,1)S(1)} collective-permute-done((bf16[32,64,128]{2,1,0:T(8,128)(2,1)S(1)}, bf16[32,64,128]{2,1,0:T(8,128)(2,1)S(1)}, u32[]{:S(2)}, u32[]{:S(2)}) %collective-permute-start.2) | collective-permute-done | bytes 524320 | tf_op jit(solution)/shard_map/ppermute | solution.py:549
  32.5 16.5 %attend.1.after_ref = bf16[32,32,128]{2,1,0:T(8,128)(2,1)S(1)} custom-call(bf16[32,96,128]{2,1,0:T(8,128)(2,1)S(1)} %all-to-all-done.own_ref, bf16[32,64,128]{2,1,0:T(8,128)(2,1)S(1)} %collective-permute-done.2.other_ref), custom_call_target="tpu_custom_call" | custom-call | tf_op jit(solution)/shard_map/attend/pallas_call | solution.py:296
  49.1 0.0 copy-start
  49.1 0.1 fusion
  49.2 0.1 select_bitcast_fusion.1
  49.2 0.1 pad_maximum_fusion
  49.3 0.9 copy.19
  50.1 5.5 %all-to-all-start.1 = ((bf16[32,2,32,128]{3,2,1,0:T(8,128)(2,1)}), bf16[32,2,32,128]{3,2,1,0:T(8,128)(2,1)S(1)}, u32[]{:S(2)}, u32[]{:S(2)}) async-start(bf16[32,2,32,128]{3,2,1,0:T(8,128)(2,1)} %copy.19), calls=%async_computation.1 | async-start | bytes 1048576 | tf_op jit(solution)/shard_map/all_to_all | solution.py:559
  55.7 0.0 copy-done.7
  55.7 0.6 reshape.21.bias_one_ref
  56.3 0.0 copy-done.8
  56.3 0.6 reshape.22.bias_two_ref
  56.9 0.0 copy-done.4
  56.9 0.6 reshape.19.gain_ref
  57.5 0.0 copy-done.5
  57.5 0.6 reshape.20.shift_ref
  58.1 0.0 copy-done.6
  58.1 0.8 reshape.24.final_bias_ref
  58.9 0.6 add_convert_fusion.inside_ref
  59.5 0.0 copy-done
  59.5 5.2 %reorder_taps.4.last_taps_ref = bf16[1,4,384,1920]{3,2,1,0:T(8,128)(2,1)} custom-call(bf16[384,4,4,1920]{3,2,1,0:T(4,128)(2,1)} %weight_ref.4, bf16[32,32,128]{2,1,0:T(8,128)(2,1)} %copy-done), custom_call_target="tpu_custom_call" | custom-call | bytes 11796480 | tf_op jit(solution)/shard_map/reorder_taps/pallas_call | solution.py:210
  64.7 0.0 copy-done.2
  64.7 0.0 copy-done.3
  64.7 5.7 %reorder_taps.5.taps_two_ref = bf16[4,4,384,384]{3,2,1,0:T(8,128)(2,1)} custom-call(bf16[384,4,4,384]{3,2,1,0:T(4,128)(2,1)} %weight_ref.5, bf16[32,32,128]{2,1,0:T(8,128)(2,1)} %copy-done), custom_call_target="tpu_custom_call" | custom-call | bytes 9437184 | tf_op jit(solution)/shard_map/reorder_taps/pallas_call | solution.py:210
  70.3 0.9 all-to-all-done.1
  71.2 0.0 copy-start.1
  71.2 0.8 copy-done.1
  72.0 22.2 %keypoint_head.1 = bf16[8,308,256]{2,1,0:T(8,128)(2,1)} custom-call(s32[2]{0:T(128)} %add_convert_fusion.inside_ref, bf16[16,2,2,32,128]{4,3,2,1,0:T(8,128)(2,1)} %bitcast.13, bf16[2,64,1920]{2,1,0:T(8,128)(2,1)} %bitcast.14, bf16[64,1920]{1,0:T(8,128)(2,1)} %copy-done.2, bf16[64,1920]{1,0:T(8,128)(2,1)} %copy-done.3, bf16[1024,1920]{1,0:T(8,128)(2,1)} %out_weight_ref.1, ...), custom_call_target="tpu_custom_call" | custom-call | tf_op jit(solution)/shard_map/keypoint_head/pallas_call | solution.py:485
  94.3 2.6 %copy.21 = bf16[1,8,256,308]{2,1,3,0:T(8,128)(2,1)} copy(bf16[1,8,256,308]{2,3,1,0:T(8,128)(2,1)} %bitcast.12) | data formatting | bytes 2523136 | tf_op jit(solution)/shard_map/broadcast_in_dim | solution.py:580
Async XLA Ops:
  2.6 27.9 %all-to-all-start = ((bf16[32,96,128]{2,1,0:T(8,128)(2,1)}), bf16[32,96,128]{2,1,0:T(8,128)(2,1)S(1)}, u32[]{:S(2)}, u32[]{:S(2)}) async-start(bf16[32,96,128]{2,1,0:T(8,128)(2,1)} %get-tuple-element.12.after_ref), calls=%async_computation | async-start | bytes 1572864 | tf_op jit(solution)/shard_map/all_to_all | solution.py:544
  9.9 18.1 %collective-permute-start = (bf16[64,1920]{1,0:T(8,128)(2,1)}, bf16[64,1920]{1,0:T(8,128)(2,1)S(1)}, u32[]{:S(2)}, u32[]{:S(2)}) collective-permute-start(bf16[64,1920]{1,0:T(8,128)(2,1)} %get-tuple-element.13), channel_id=1, source_target_pairs={{0,1},{1,2},{2,3},{3,4},{4,5},{5,6},{6,7},{7,8},{8,9},{9,10},{10,1... | collective-permute-start | bytes 737288 | tf_op jit(solution)/shard_map/ppermute | solution.py:545
  12.1 16.0 %collective-permute-start.1 = (bf16[64,1920]{1,0:T(8,128)(2,1)}, bf16[64,1920]{1,0:T(8,128)(2,1)S(1)}, u32[]{:S(2)}, u32[]{:S(2)}) collective-permute-start(bf16[64,1920]{1,0:T(8,128)(2,1)} %get-tuple-element.14), channel_id=1, source_target_pairs={{1,0},{2,1},{3,2},{4,3},{5,4},{6,5},{7,6},{8,7},{9,8},{10,9},{11,1... | collective-permute-start | bytes 737288 | tf_op jit(solution)/shard_map/ppermute | solution.py:546
  28.0 27.7 %copy-start.7 = (f32[384]{0:T(512)S(1)}, f32[384]{0:T(512)}, u32[]{:S(2)}) copy-start(f32[384]{0:T(512)} %param.21) | copy-start | bytes 4612
  28.0 28.3 %copy-start.8 = (f32[384]{0:T(512)S(1)}, f32[384]{0:T(512)}, u32[]{:S(2)}) copy-start(f32[384]{0:T(512)} %param.23) | copy-start | bytes 4612
  28.0 28.9 %copy-start.4 = (f32[1920]{0:T(1024)S(1)}, f32[1920]{0:T(1024)}, u32[]{:S(2)}) copy-start(f32[1920]{0:T(1024)} %param.18) | copy-start | bytes 23044
  28.0 29.5 %copy-start.5 = (f32[1920]{0:T(1024)S(1)}, f32[1920]{0:T(1024)}, u32[]{:S(2)}) copy-start(f32[1920]{0:T(1024)} %param.19) | copy-start | bytes 23044
  28.0 30.1 %copy-start.6 = (f32[308]{0:T(512)S(1)}, f32[308]{0:T(512)}, u32[]{:S(2)}) copy-start(f32[308]{0:T(512)} %param.25) | copy-start | bytes 3700
  28.0 36.6 %copy-start.2 = (bf16[64,1920]{1,0:T(8,128)(2,1)}, bf16[64,1920]{1,0:T(8,128)(2,1)S(1)}, u32[]{:S(2)}) copy-start(bf16[64,1920]{1,0:T(8,128)(2,1)S(1)} %collective-permute-done.above_ref) | copy-start | bytes 737284
  28.1 36.6 %copy-start.3 = (bf16[64,1920]{1,0:T(8,128)(2,1)}, bf16[64,1920]{1,0:T(8,128)(2,1)S(1)}, u32[]{:S(2)}) copy-start(bf16[64,1920]{1,0:T(8,128)(2,1)S(1)} %collective-permute-done.1.below_ref) | copy-start | bytes 737284
  30.6 2.0 %collective-permute-start.2 = (bf16[32,64,128]{2,1,0:T(8,128)(2,1)S(1)}, bf16[32,64,128]{2,1,0:T(8,128)(2,1)S(1)}, u32[]{:S(2)}, u32[]{:S(2)}) collective-permute-start(bf16[32,64,128]{2,1,0:T(8,128)(2,1)S(1)} %slice.9), channel_id=1, source_target_pairs={{0,1},{1,0},{2,3},{3,2},{4,5},{5,4},{6,7},{7,6},{8,9},{9,8},{10,11... | collective-permute-start | bytes 1572872 | tf_op jit(solution)/shard_map/ppermute | solution.py:549
  49.1 10.4 %copy-start = (bf16[32,32,128]{2,1,0:T(8,128)(2,1)}, bf16[32,32,128]{2,1,0:T(8,128)(2,1)S(1)}, u32[]{:S(2)}) copy-start(bf16[32,32,128]{2,1,0:T(8,128)(2,1)S(1)} %attend.1.after_ref) | copy-start | bytes 786436
  50.1 21.1 %all-to-all-start.1 = ((bf16[32,2,32,128]{3,2,1,0:T(8,128)(2,1)}), bf16[32,2,32,128]{3,2,1,0:T(8,128)(2,1)S(1)}, u32[]{:S(2)}, u32[]{:S(2)}) async-start(bf16[32,2,32,128]{3,2,1,0:T(8,128)(2,1)} %copy.19), calls=%async_computation.1 | async-start | bytes 1048576 | tf_op jit(solution)/shard_map/all_to_all | solution.py:559
  71.2 0.8 copy-start.1
where the time goes:
time: 97.4 us; the launch traced here: 96.8 us
  Pallas kernels  66.8 us (69%)
  starting transfers between devices  16.3 us (17%)
  local copies, waits for them, and re-layouts  7.57 us (8%)
  waiting for transfers between devices  5.22 us (5%)
    pallas_call x3, Pallas kernels, reorder_taps(): pl.pallas_call(reorder_kernel, grid=(len(rows), channels // block), in_sp...  25.5 us
    pallas_call x1, Pallas kernels, keypoint_head(): pl.pallas_call(head_kernel, in_specs=[pl.BlockSpec(memory_space=pltpu.SME...  22.2 us
    pallas_call x1, Pallas kernels, attend(): pl.pallas_call(functools.partial(attend_kernel, sources=sources, chunk=ch...  16.5 us
    all_to_all x1, starting transfers between devices, by_heads(): own = lax.all_to_all(packed, 'seq', 0, 0, tiled=True)  7.3 us
    all_to_all x1, starting transfers between devices, by_heads(): back = lax.all_to_all(sent, 'seq', 0, 0, tiled=True)  5.51 us
    broadcast_in_dim x1, local copies, waits for them, and re-layouts, by_heads(): return jnp.transpose(heat, (0, 2, 1))[None]  2.6 us
    pallas_call x1, Pallas kernels, pack_tokens(): pl.pallas_call(pack_kernel, in_specs=[pl.BlockSpec(memory_space=pl.ANY)]...  2.57 us
    all_to_all x1, waiting for transfers between devices, by_heads(): own = lax.all_to_all(packed, 'seq', 0, 0, tiled=True)  2.44 us
  transfers between devices with their start and end apart: 5, of which 3 were waited for; matrix products, arithmetic and copies ran while one was open for 4% of the time, Pallas kernels for 26%

commit v1 on v0

--- a/solution.py
+++ b/solution.py
@@ -222,7 +222,34 @@
     )(weight, after)
 
 
-def attend_kernel(own_ref, other_ref, out_ref, pairs_ref, values_ref, top_ref, total_ref, mixed_ref, *, sources, chunk):
+def pair_kernel(weight_ref, after_ref, out_ref):
+    del after_ref
+    width = weight_ref.shape[3]
+    taps = jnp.swapaxes(weight_ref[:, 0], 0, 1)
+    for parity, columns in enumerate(((3, 1), (2, 0))):
+        for place, column in enumerate(columns):
+            out_ref[0, parity, :, place * width : (place + 1) * width] = taps[column]
+
+
+def pair_taps(weight, after):
+    channels, rows, columns, width = weight.shape
+    moved = 2 * channels * rows * columns * width * weight.dtype.itemsize
+    return pl.pallas_call(
+        pair_kernel,
+        grid=(rows,),
+        in_specs=[
+            pl.BlockSpec((channels, 1, columns, width), lambda i: (0, i, 0, 0)),
+            pl.BlockSpec(memory_space=pl.ANY),
+        ],
+        out_specs=pl.BlockSpec((1, 2, channels, 2 * width), lambda i: (i, 0, 0, 0)),
+        out_shape=jax.ShapeDtypeStruct((rows, 2, channels, 2 * width), weight.dtype),
+        compiler_params=pltpu.CompilerParams(vmem_limit_bytes=60 * MIB),
+        cost_estimate=pl.CostEstimate(flops=0, bytes_accessed=moved, transcendentals=0),
+        name="pair_taps",
+    )(weight, after)
+
+
+def attend_kernel(parity_ref, own_ref, other_ref, out_ref, pairs_ref, values_ref, top_ref, total_ref, mixed_ref, *, sources, chunk):
     half = pairs_ref.shape[0] // 2
     count = 2 * half
 
@@ -288,17 +315,40 @@
 
     attended = mixed_ref[...] / total_ref[...]
     joined = jnp.concatenate([attended[:, :rows], attended[:, rows:]], axis=0)
-    out_ref[...] = joined.T.astype(jnp.bfloat16).reshape(sources, 32, 128)
-
-
-def attend(own, other, sources=16, chunk=512):
+    rows = joined.T.astype(jnp.bfloat16).reshape(sources, 32, 128)
+    steps = out_ref.shape[0] // sources
+    rim = jnp.zeros((32, 128), jnp.bfloat16)
+    for step in range(steps):
+        start, stop = step * sources, (step + 1) * sources
+
+        @pl.when((pl.program_id(0) == step) & (parity_ref[0] == 0))
+        def _():
+            out_ref[start:stop, 0] = rows
+            if step == 0:
+                out_ref[0 : stop - 1, 1] = rows[1:]
+                out_ref[steps * sources - 1, 1] = rim
+            else:
+                out_ref[start - 1 : stop - 1, 1] = rows
+
+        @pl.when((pl.program_id(0) == step) & (parity_ref[0] == 1))
+        def _():
+            out_ref[start:stop, 1] = rows
+            if step == 0:
+                out_ref[0, 0] = rim
+            if step == steps - 1:
+                out_ref[start + 1 : stop, 0] = rows[:-1]
+            else:
+                out_ref[start + 1 : stop + 1, 0] = rows
+
+
+def attend(parity, own, other, sources=16, chunk=512):
     count = own.shape[0]
     return pl.pallas_call(
         functools.partial(attend_kernel, sources=sources, chunk=chunk),
         grid=(count // sources,),
-        in_specs=[whole(own.shape), whole(other.shape)],
-        out_specs=pl.BlockSpec((sources, 32, 128), lambda i: (i, 0, 0)),
-        out_shape=jax.ShapeDtypeStruct((count, 32, 128), jnp.bfloat16),
+        in_specs=[pl.BlockSpec(memory_space=pltpu.SMEM), whole(own.shape), whole(other.shape)],
+        out_specs=whole((count, 2, 32, 128)),
+        out_shape=jax.ShapeDtypeStruct((count, 2, 32, 128), jnp.bfloat16),
         scratch_shapes=[
             pltpu.VMEM((2 * count * 64, 128), jnp.bfloat16),
             pltpu.VMEM((64, 2 * count * 64), jnp.bfloat16),
@@ -308,7 +358,7 @@
         ],
         compiler_params=pltpu.CompilerParams(vmem_limit_bytes=40 * MIB),
         name="attend",
-    )(own, other)
+    )(parity, own, other)
 
 
 def shift_columns(field, row_length):
@@ -328,10 +378,6 @@
 def load_wide(wide_ref, rows):
     groups = [wide_ref[group, rows, :] for group in range(wide_ref.shape[0])]
     return jnp.concatenate(groups, axis=1).astype(jnp.bfloat16)
-
-
-def column_taps(parity):
-    return ((1, 1), (0, 3)) if parity == 0 else ((1, 2), (2, 0))
 
 
 def attended_rows(mixed_ref):
@@ -371,18 +417,17 @@
     wide_one_ref,
     copies_ref,
     wide_two_ref,
+    heat_ref,
     done,
 ):
-    channels = bias_one_ref.shape[1]
-    order = ((1, 0), (1, 1), (3, 0), (3, 1), (2, 0), (2, 1), (0, 0), (0, 1))
+    channels = bias_one_ref.shape[0]
     slots = weight_one_ref.shape[0]
     ahead = slots - 1
     first = pltpu.make_async_copy(out_weight_ref, projection_ref, done.at[0])
     last = pltpu.make_async_copy(taps_two_ref, weight_two_ref, done.at[1])
     copies = []
-    for index, (_, half) in enumerate(order):
-        taps = first_taps_ref.at[index // 2] if index < 6 else last_taps_ref.at[0]
-        source = taps.at[pl.ds(2 * half, 2)]
+    for index in range(4):
+        source = first_taps_ref.at[index] if index < 3 else last_taps_ref.at[0]
         slot = index % slots
         copies.append(pltpu.make_async_copy(source, weight_one_ref.at[slot], done.at[2 + index]))
     first.start()
@@ -390,8 +435,9 @@
 
     attended = attended_rows(mixed_ref)
     first.wait()
-    for copy in copies[1:ahead]:
+    for copy in copies[1:]:
         copy.start()
+    last.start()
     projected = jnp.dot(attended, projection_ref[...], preferred_element_type=jnp.float32)
     for place, resid in enumerate((above_ref[...], resid_ref[0], resid_ref[1], below_ref[...])):
         rows = slice(64 * place, 64 * place + 64)
@@ -399,36 +445,29 @@
         center = jnp.mean(stream, axis=-1, keepdims=True)
         shifted = stream - center
         variance = jnp.mean(shifted * shifted, axis=-1, keepdims=True)
-        normed = shifted * lax.rsqrt(variance + EPSILON) * gain_ref[...] + shift_ref[...]
+        normed = shifted * lax.rsqrt(variance + EPSILON) * gain_ref[...][None, :] + shift_ref[...][None, :]
         if place in (0, 3):
             normed = jnp.where(inside_ref[place // 3] > 0, normed, 0.0)
         field_ref[rows, :] = normed.astype(jnp.bfloat16)
 
-    for index, (kernel_row, half) in enumerate(order):
+    for index, kernel_row in enumerate((1, 3, 2, 0)):
         copies[index].wait()
-        if index + ahead < len(order):
-            copies[index + ahead].start()
-        elif index + ahead == len(order):
-            last.start()
+        if index == 3:
+            last.wait()
         low = 64 if kernel_row < 2 else 0
-        weight = weight_one_ref[index % slots].reshape(2 * channels, weight_one_ref.shape[3])
+        weight = weight_one_ref[index % slots].reshape(4 * channels, weight_one_ref.shape[3])
         product = dot_nt(field_ref[low : low + 192, :], weight)
-        odd, even = product[:, :channels], product[:, channels:]
-        if half == 0:
-            odd = shift_columns(odd, 64)[1]
-        else:
-            even = shift_columns(even, 64)[0]
-        if index % 4 == 0:
+        parts = [product[:, channels * column : channels * (column + 1)] for column in range(4)]
+        odd = shift_columns(parts[0], 64)[1] + parts[2]
+        even = shift_columns(parts[3], 64)[0] + parts[1]
+        if index % 2 == 0:
             sums_ref[0] = even
             sums_ref[1] = odd
         else:
-            sums_ref[0] += even
-            sums_ref[1] += odd
-        if index % 4 == 3:
             for parity in range(2):
-                hidden = jnp.maximum(sums_ref[parity] + bias_one_ref[...], 0.0)
+                hidden = jnp.maximum((even, odd)[parity] + sums_ref[parity] + bias_one_ref[...][None, :], 0.0)
                 for place in range(3):
-                    row = 2 * place + (1 if index == 3 else 0)
+                    row = 2 * place + (1 if index == 1 else 0)
                     value = hidden[64 * place : 64 * place + 64]
                     if row in (0, 5):
                         value = jnp.where(inside_ref[row // 5] > 0, value, 0.0)
@@ -439,25 +478,22 @@
     copies_ref[:, 0:channels] = before.astype(jnp.bfloat16)
     copies_ref[:, channels : 2 * channels] = hidden
     copies_ref[:, 2 * channels :] = after.astype(jnp.bfloat16)
-    last.wait()
     for row_parity in range(2):
         for parity in range(2):
             total = None
+            lanes = slice(parity * channels, (parity + 2) * channels)
             for low, kernel_row in (((128, 1), (0, 3)), ((128, 2), (256, 0)))[row_parity]:
-                for copy, kernel_col in column_taps(parity):
-                    product = dot_nt(
-                        copies_ref[low : low + 512, copy * channels : (copy + 1) * channels],
-                        weight_two_ref[kernel_row, kernel_col],
-                    )
-                    total = product if total is None else total + product
-            hidden = jnp.maximum(total + bias_two_ref[...], 0.0)
+                product = dot_nt(copies_ref[low : low + 512, lanes], weight_two_ref[kernel_row, parity])
+                total = product if total is None else total + product
+            hidden = jnp.maximum(total + bias_two_ref[...][None, :], 0.0)
             for place in range(4):
                 start = 256 * (2 * place + row_parity) + parity
                 store_strided(wide_two_ref, start, hidden[128 * place : 128 * place + 128])
     for row in range(8):
         hidden = load_wide(wide_two_ref, slice(256 * row, 256 * row + 256))
         heat = dot_nt(final_ref[...], hidden) + final_bias_ref[...]
-        out_ref[row] = heat.astype(jnp.bfloat16)
+        heat_ref[row] = heat.astype(jnp.bfloat16)
+    out_ref[...] = jnp.swapaxes(heat_ref[...], 0, 1)
 
 
 def keypoint_head(
@@ -486,17 +522,18 @@
         head_kernel,
         in_specs=[pl.BlockSpec(memory_space=pltpu.SMEM), near, near, near, near, far, near, near]
         + [far, far, near, far, near, near, near],
-        out_shape=jax.ShapeDtypeStruct((8, keypoints, 256), jnp.bfloat16),
+        out_shape=jax.ShapeDtypeStruct((keypoints, 8, 256), jnp.bfloat16),
         scratch_shapes=[
             pltpu.VMEM(out_weight.shape, jnp.bfloat16),
-            pltpu.VMEM((5, 2, channels, width), jnp.bfloat16),
-            pltpu.VMEM((4, 4, channels, channels), jnp.bfloat16),
+            pltpu.VMEM((4, 4, channels, width), jnp.bfloat16),
+            pltpu.VMEM((4, 2, channels, 2 * channels), jnp.bfloat16),
             pltpu.VMEM((256, width), jnp.bfloat16),
             pltpu.VMEM((2, 192, channels), jnp.float32),
             pltpu.VMEM((channels // 128, 768, 128), jnp.float32),
             pltpu.VMEM((768, 3 * channels), jnp.bfloat16),
             pltpu.VMEM((channels // 128, 2048, 128), jnp.float32),
-            pltpu.SemaphoreType.DMA((10,)),
+            pltpu.VMEM((8, keypoints, 256), jnp.bfloat16),
+            pltpu.SemaphoreType.DMA((6,)),
         ],
         compiler_params=pltpu.CompilerParams(vmem_limit_bytes=57 * MIB + MIB // 2),
         name="keypoint_head",
@@ -507,13 +544,13 @@
         above,
         below,
         out_weight,
-        gain.reshape(1, -1),
-        shift.reshape(1, -1),
+        gain,
+        shift,
         first_taps,
         last_taps,
-        bias_one.reshape(1, -1),
+        bias_one,
         taps_two,
-        bias_two.reshape(1, -1),
+        bias_two,
         final_weight.T,
         final_bias.reshape(-1, 1),
     )
@@ -547,15 +584,9 @@
     first_taps = reorder_taps(deconv1_weight, (1, 3, 2), packed)
     own, above, below, first_taps = lax.optimization_barrier((own, above, below, first_taps))
     other = lax.ppermute(own[:, 32:96], "seq", swap)
-    mixed = attend(own, other)
-    last_taps = reorder_taps(deconv1_weight, (0,), mixed)
-    taps_two = reorder_taps(deconv2_weight, (0, 1, 2, 3), mixed)
-
-    rim = jnp.zeros((1, 32, 128), jnp.bfloat16)
-    earlier = jnp.concatenate([rim, mixed[:-1]], axis=0)
-    later = jnp.concatenate([mixed[1:], rim], axis=0)
-    odd = place % 2 == 1
-    sent = jnp.stack([jnp.where(odd, earlier, mixed), jnp.where(odd, mixed, later)], axis=1)
+    sent = attend((place % 2).astype(jnp.int32).reshape(1), own, other)
+    last_taps = reorder_taps(deconv1_weight, (0,), sent)
+    taps_two = pair_taps(deconv2_weight, sent)
     back = lax.all_to_all(sent, "seq", 0, 0, tiled=True)
     back = back.reshape(count // 2, 2, 2, 32, 128)
 
@@ -577,7 +608,7 @@
         final_weight,
         final_bias,
     )
-    return jnp.transpose(heat, (0, 2, 1))[None]
+    return jnp.transpose(heat, (1, 2, 0))[None]
 
 
 def step(*arrays):

time: 97.4 us -> 92.1 us (0.946)
  local copies, waits for them, and re-layouts: 7.57 us -> 1.64 us
  waiting for transfers between devices: 5.22 us -> 7.78 us
  Pallas kernels: 66.8 us -> 65 us
    pallas_call x3 -> x2, Pallas kernels: 25.5 us -> 19.8 us  [reorder_taps(): pl.pallas_call(reorder_kernel, grid=(len(rows), channels // block), in_sp...]
    pallas_call x0 -> x1, Pallas kernels: none -> 5.6 us  [pair_taps(): pl.pallas_call(pair_kernel, grid=(rows,), in_specs=[pl.BlockSpec((channel...]
    pallas_call x1, Pallas kernels: 22.2 us -> 19.6 us  [keypoint_head(): pl.pallas_call(head_kernel, in_specs=[pl.BlockSpec(memory_space=pltpu.SME...]
    broadcast_in_dim x1 -> x0, local copies, waits for them, and re-layouts: 2.6 us -> none  [by_heads(): return jnp.transpose(heat, (0, 2, 1))[None]]
    all_to_all x1, waiting for transfers between devices: 0.89 us -> 3.42 us  [by_heads(): back = lax.all_to_all(sent, 'seq', 0, 0, tiled=True)]
    reshape x4 -> x0, local copies, waits for them, and re-layouts: 2.4 us -> none  [the longest x1 0.61 us: keypoint_head(): shift.reshape(1, -1)]
  transfers between devices with their start and end apart: 5 -> 5, of which waited for: 3 -> 3; matrix products, arithmetic and copies ran while one was open for 4% -> 1% of each run, Pallas kernels for 26% -> 28%
where the time goes in v1:
time: 92.1 us; the launch traced here: 91.6 us
  Pallas kernels  65 us (71%)
  starting transfers between devices  16.3 us (18%)
  waiting for transfers between devices  7.78 us (8%)
  local copies, waits for them, and re-layouts  1.64 us (2%)
    pallas_call x2, Pallas kernels, reorder_taps(): pl.pallas_call(reorder_kernel, grid=(len(rows), channels // block), in_sp...  19.8 us
    pallas_call x1, Pallas kernels, keypoint_head(): pl.pallas_call(head_kernel, in_specs=[pl.BlockSpec(memory_space=pltpu.SME...  19.6 us
    pallas_call x1, Pallas kernels, attend(): pl.pallas_call(functools.partial(attend_kernel, sources=sources, chunk=ch...  17.4 us
    all_to_all x1, starting transfers between devices, by_heads(): own = lax.all_to_all(packed, 'seq', 0, 0, tiled=True)  7.3 us
    pallas_call x1, Pallas kernels, pair_taps(): pl.pallas_call(pair_kernel, grid=(rows,), in_specs=[pl.BlockSpec((channel...  5.6 us
    all_to_all x1, starting transfers between devices, by_heads(): back = lax.all_to_all(sent, 'seq', 0, 0, tiled=True)  5.48 us
    all_to_all x1, waiting for transfers between devices, by_heads(): back = lax.all_to_all(sent, 'seq', 0, 0, tiled=True)  3.42 us
    pallas_call x1, Pallas kernels, pack_tokens(): pl.pallas_call(pack_kernel, in_specs=[pl.BlockSpec(memory_space=pl.ANY)]...  2.59 us
  transfers between devices with their start and end apart: 5, of which 3 were waited for; matrix products, arithmetic and copies ran while one was open for 1% of the time, Pallas kernels for 28%

profile of v1, /device:TPU:0, one launch (start us, length us, event | category | flops | bytes accessed | tf_op | source)
XLA Modules:
  0.0 91.6 jit_solution(167478688298535701)
XLA Ops:
  0.0 2.6 %pack_tokens.1 = (bf16[32,96,128]{2,1,0:T(8,128)(2,1)}, bf16[64,1920]{1,0:T(8,128)(2,1)}, bf16[64,1920]{1,0:T(8,128)(2,1)}) custom-call(bf16[1,2,64,1024]{3,2,1,0:T(8,128)(2,1)} %query_ref.1, bf16[1,2,64,1024]{3,2,1,0:T(8,128)(2,1)} %keys_ref.1, bf16[1,2,64,1024]{3,2,1,0:T(8,128)(2,1)} %values_ref.1, bf16[1,2,64,1920]{3,2,1,0:T(8,128)(2,1)} %resid_ref.1), custom_call_target="tpu_custom_call" | custom-call | tf_op jit(solution)/shard_map/pack_tokens/pallas_call | solution.py:184
  2.6 7.3 %all-to-all-start = ((bf16[32,96,128]{2,1,0:T(8,128)(2,1)}), bf16[32,96,128]{2,1,0:T(8,128)(2,1)S(1)}, u32[]{:S(2)}, u32[]{:S(2)}) async-start(bf16[32,96,128]{2,1,0:T(8,128)(2,1)} %get-tuple-element.12.after_ref), calls=%async_computation | async-start | bytes 1572864 | tf_op jit(solution)/shard_map/all_to_all | solution.py:581
  9.9 2.2 %collective-permute-start = (bf16[64,1920]{1,0:T(8,128)(2,1)}, bf16[64,1920]{1,0:T(8,128)(2,1)S(1)}, u32[]{:S(2)}, u32[]{:S(2)}) collective-permute-start(bf16[64,1920]{1,0:T(8,128)(2,1)} %get-tuple-element.13), channel_id=1, source_target_pairs={{0,1},{1,2},{2,3},{3,4},{4,5},{5,6},{6,7},{7,8},{8,9},{9,10},{10,1... | collective-permute-start | bytes 737288 | tf_op jit(solution)/shard_map/ppermute | solution.py:582
  12.1 0.0 copy-start.3
  12.1 1.3 %collective-permute-start.1 = (bf16[64,1920]{1,0:T(8,128)(2,1)}, bf16[64,1920]{1,0:T(8,128)(2,1)S(1)}, u32[]{:S(2)}, u32[]{:S(2)}) collective-permute-start(bf16[64,1920]{1,0:T(8,128)(2,1)} %get-tuple-element.14), channel_id=1, source_target_pairs={{1,0},{2,1},{3,2},{4,3},{5,4},{6,5},{7,6},{8,7},{9,8},{10,9},{11,1... | collective-permute-start | bytes 737288 | tf_op jit(solution)/shard_map/ppermute | solution.py:583
  13.4 14.6 %reorder_taps.2.first_taps_ref = bf16[3,4,384,1920]{3,2,1,0:T(8,128)(2,1)} custom-call(bf16[384,4,4,1920]{3,2,1,0:T(4,128)(2,1)} %weight_ref.4, bf16[32,96,128]{2,1,0:T(8,128)(2,1)} %get-tuple-element.12.after_ref), custom_call_target="tpu_custom_call" | custom-call | bytes 35389440 | tf_op jit(solution)/shard_map/reorder_taps/pallas_call | solution.py:210
  28.0 0.0 collective-permute-done.above_ref
  28.1 0.0 copy-start.1
  28.1 0.0 collective-permute-done.1.below_ref
  28.1 0.0 copy-start.2
  28.1 2.5 %all-to-all-done.own_ref = bf16[32,96,128]{2,1,0:T(8,128)(2,1)S(1)} async-done(((bf16[32,96,128]{2,1,0:T(8,128)(2,1)}), bf16[32,96,128]{2,1,0:T(8,128)(2,1)S(1)}, u32[]{:S(2)}, u32[]{:S(2)}) %all-to-all-start) | async-done | bytes 786464 | tf_op jit(solution)/shard_map/all_to_all | solution.py:581
  30.5 0.1 slice.3
  30.6 0.1 collective-permute-start.2
  30.7 1.9 %collective-permute-done.2.other_ref = bf16[32,64,128]{2,1,0:T(8,128)(2,1)S(1)} collective-permute-done((bf16[32,64,128]{2,1,0:T(8,128)(2,1)S(1)}, bf16[32,64,128]{2,1,0:T(8,128)(2,1)S(1)}, u32[]{:S(2)}, u32[]{:S(2)}) %collective-permute-start.2) | collective-permute-done | bytes 524320 | tf_op jit(solution)/shard_map/ppermute | solution.py:586
  32.6 17.4 %attend.1.after_ref = bf16[32,2,32,128]{3,2,1,0:T(8,128)(2,1)} custom-call(s32[1]{0:T(128)} %bitcast.2.parity_ref, bf16[32,96,128]{2,1,0:T(8,128)(2,1)S(1)} %all-to-all-done.own_ref, bf16[32,64,128]{2,1,0:T(8,128)(2,1)S(1)} %collective-permute-done.2.other_ref), custom_call_target="tpu_custom_call" | custom-call | tf_op jit(solution)/shard_map/attend/pallas_call | solution.py:346
  50.0 5.5 %all-to-all-start.1 = ((bf16[32,2,32,128]{3,2,1,0:T(8,128)(2,1)}), bf16[32,2,32,128]{3,2,1,0:T(8,128)(2,1)S(1)}, u32[]{:S(2)}, u32[]{:S(2)}) async-start(bf16[32,2,32,128]{3,2,1,0:T(8,128)(2,1)} %attend.1.after_ref), calls=%async_computation.1 | async-start | bytes 1048576 | tf_op jit(solution)/shard_map/all_to_all | solution.py:590
  55.5 0.0 copy-done.3
  55.5 0.8 reshape.12.final_bias_ref
  56.3 0.6 add_convert_fusion.inside_ref
  56.9 5.1 %reorder_taps.3.last_taps_ref = bf16[1,4,384,1920]{3,2,1,0:T(8,128)(2,1)} custom-call(bf16[384,4,4,1920]{3,2,1,0:T(4,128)(2,1)} %weight_ref.4, bf16[32,2,32,128]{3,2,1,0:T(8,128)(2,1)} %attend.1.after_ref), custom_call_target="tpu_custom_call" | custom-call | bytes 11796480 | tf_op jit(solution)/shard_map/reorder_taps/pallas_call | solution.py:210
  62.0 0.0 copy-done.1
  62.0 0.0 copy-done.2
  62.0 5.6 %pair_taps.1.taps_two_ref = bf16[4,2,384,768]{3,2,1,0:T(8,128)(2,1)} custom-call(bf16[384,4,4,384]{3,2,1,0:T(4,128)(2,1)} %weight_ref.5, bf16[32,2,32,128]{3,2,1,0:T(8,128)(2,1)} %attend.1.after_ref), custom_call_target="tpu_custom_call" | custom-call | bytes 9437184 | tf_op jit(solution)/shard_map/pair_taps/pallas_call | solution.py:237
  67.6 3.4 %all-to-all-done.1 = bf16[32,2,32,128]{3,2,1,0:T(8,128)(2,1)S(1)} async-done(((bf16[32,2,32,128]{3,2,1,0:T(8,128)(2,1)}), bf16[32,2,32,128]{3,2,1,0:T(8,128)(2,1)S(1)}, u32[]{:S(2)}, u32[]{:S(2)}) %all-to-all-start.1) | async-done | bytes 524320 | tf_op jit(solution)/shard_map/all_to_all | solution.py:590
  71.0 0.0 copy-start
  71.0 0.8 copy-done
  71.8 19.6 %keypoint_head.1 = bf16[308,8,256]{2,1,0:T(8,128)(2,1)} custom-call(s32[2]{0:T(128)} %add_convert_fusion.inside_ref, bf16[16,2,2,32,128]{4,3,2,1,0:T(8,128)(2,1)} %bitcast.9, bf16[2,64,1920]{2,1,0:T(8,128)(2,1)} %bitcast.10, bf16[64,1920]{1,0:T(8,128)(2,1)} %copy-done.1, bf16[64,1920]{1,0:T(8,128)(2,1)} %copy-done.2, bf16[1024,1920]{1,0:T(8,128)(2,1)} %out_weight_ref.1, ...), custom_call_target="tpu_custom_call" | custom-call | tf_op jit(solution)/shard_map/keypoint_head/pallas_call | solution.py:521
Async XLA Ops:
  2.6 27.9 %all-to-all-start = ((bf16[32,96,128]{2,1,0:T(8,128)(2,1)}), bf16[32,96,128]{2,1,0:T(8,128)(2,1)S(1)}, u32[]{:S(2)}, u32[]{:S(2)}) async-start(bf16[32,96,128]{2,1,0:T(8,128)(2,1)} %get-tuple-element.12.after_ref), calls=%async_computation | async-start | bytes 1572864 | tf_op jit(solution)/shard_map/all_to_all | solution.py:581
  9.9 18.1 %collective-permute-start = (bf16[64,1920]{1,0:T(8,128)(2,1)}, bf16[64,1920]{1,0:T(8,128)(2,1)S(1)}, u32[]{:S(2)}, u32[]{:S(2)}) collective-permute-start(bf16[64,1920]{1,0:T(8,128)(2,1)} %get-tuple-element.13), channel_id=1, source_target_pairs={{0,1},{1,2},{2,3},{3,4},{4,5},{5,6},{6,7},{7,8},{8,9},{9,10},{10,1... | collective-permute-start | bytes 737288 | tf_op jit(solution)/shard_map/ppermute | solution.py:582
  12.1 43.4 %copy-start.3 = (f32[308]{0:T(512)S(1)}, f32[308]{0:T(512)}, u32[]{:S(2)}) copy-start(f32[308]{0:T(512)} %param.25) | copy-start | bytes 3700
  12.1 16.0 %collective-permute-start.1 = (bf16[64,1920]{1,0:T(8,128)(2,1)}, bf16[64,1920]{1,0:T(8,128)(2,1)S(1)}, u32[]{:S(2)}, u32[]{:S(2)}) collective-permute-start(bf16[64,1920]{1,0:T(8,128)(2,1)} %get-tuple-element.14), channel_id=1, source_target_pairs={{1,0},{2,1},{3,2},{4,3},{5,4},{6,5},{7,6},{8,7},{9,8},{10,9},{11,1... | collective-permute-start | bytes 737288 | tf_op jit(solution)/shard_map/ppermute | solution.py:583
  28.1 33.9 %copy-start.1 = (bf16[64,1920]{1,0:T(8,128)(2,1)}, bf16[64,1920]{1,0:T(8,128)(2,1)S(1)}, u32[]{:S(2)}) copy-start(bf16[64,1920]{1,0:T(8,128)(2,1)S(1)} %collective-permute-done.above_ref) | copy-start | bytes 737284
  28.1 33.9 %copy-start.2 = (bf16[64,1920]{1,0:T(8,128)(2,1)}, bf16[64,1920]{1,0:T(8,128)(2,1)S(1)}, u32[]{:S(2)}) copy-start(bf16[64,1920]{1,0:T(8,128)(2,1)S(1)} %collective-permute-done.1.below_ref) | copy-start | bytes 737284
  30.6 2.0 %collective-permute-start.2 = (bf16[32,64,128]{2,1,0:T(8,128)(2,1)S(1)}, bf16[32,64,128]{2,1,0:T(8,128)(2,1)S(1)}, u32[]{:S(2)}, u32[]{:S(2)}) collective-permute-start(bf16[32,64,128]{2,1,0:T(8,128)(2,1)S(1)} %slice.3), channel_id=1, source_target_pairs={{0,1},{1,0},{2,3},{3,2},{4,5},{5,4},{6,7},{7,6},{8,9},{9,8},{10,11... | collective-permute-start | bytes 1572872 | tf_op jit(solution)/shard_map/ppermute | solution.py:586
  50.0 21.0 %all-to-all-start.1 = ((bf16[32,2,32,128]{3,2,1,0:T(8,128)(2,1)}), bf16[32,2,32,128]{3,2,1,0:T(8,128)(2,1)S(1)}, u32[]{:S(2)}, u32[]{:S(2)}) async-start(bf16[32,2,32,128]{3,2,1,0:T(8,128)(2,1)} %attend.1.after_ref), calls=%async_computation.1 | async-start | bytes 1048576 | tf_op jit(solution)/shard_map/all_to_all | solution.py:590
  71.0 0.8 copy-start

commit v2 on v1

--- a/solution.py
+++ b/solution.py
@@ -249,25 +249,22 @@
     )(weight, after)
 
 
-def attend_kernel(parity_ref, own_ref, other_ref, out_ref, pairs_ref, values_ref, top_ref, total_ref, mixed_ref, *, sources, chunk):
+def attend_kernel(parity_ref, own_ref, other_ref, out_ref, pairs_ref, values_ref, total_ref, mixed_ref, *, chunk):
     half = pairs_ref.shape[0] // 2
     count = 2 * half
 
-    @pl.when(pl.program_id(0) == 0)
-    def _():
-        pairs_ref[0:half, :] = own_ref[:, 32:96, :].reshape(half, 128)
-        pairs_ref[half:count, :] = other_ref[...].reshape(half, 128)
-        longest = jnp.zeros((1, 1), jnp.float32)
-        for start in range(0, count, 512):
-            wide = pairs_ref[start : start + 512, :].astype(jnp.float32).T
-            values_ref[:, start : start + 512] = wide[64:128].astype(jnp.bfloat16)
-            norms = jnp.sum(wide[0:64] * wide[0:64], axis=0, keepdims=True)
-            longest = jnp.maximum(longest, jnp.max(norms, axis=1, keepdims=True))
-        top_ref[0:1, 0:128] = jnp.broadcast_to(longest, (1, 128))
-
-    first = pl.program_id(0) * sources
+    pairs_ref[0:half, :] = own_ref[:, 32:96, :].reshape(half, 128)
+    pairs_ref[half:count, :] = other_ref[...].reshape(half, 128)
+    longest = jnp.zeros((1, 1), jnp.float32)
+    for start in range(0, count, 512):
+        wide = pairs_ref[start : start + 512, :].astype(jnp.float32).T
+        values_ref[:, start : start + 512] = wide[64:128].astype(jnp.bfloat16)
+        norms = jnp.sum(wide[0:64] * wide[0:64], axis=0, keepdims=True)
+        longest = jnp.maximum(longest, jnp.max(norms, axis=1, keepdims=True))
+
+    sources = own_ref.shape[0]
     rows = sources * 32
-    packed = own_ref[pl.ds(first, sources), 0:32, :].reshape(rows, 128)
+    packed = own_ref[:, 0:32, :].reshape(rows, 128)
     wide = (packed.astype(jnp.float32) * HEAD_DIM ** (-0.5)).T
     zeros = jnp.zeros((64, rows), jnp.float32)
     exact = jnp.concatenate(
@@ -275,7 +272,7 @@
     )
     queries = exact.astype(jnp.bfloat16)
     norms = jnp.sum(exact * exact, axis=0, keepdims=True)
-    bound = 1.01 * jnp.max(norms * top_ref[0:1, 0:1])
+    bound = 1.01 * jnp.max(norms * longest)
     small = bound <= 50.0 * 50.0
 
     @pl.when(small)
@@ -316,45 +313,30 @@
     attended = mixed_ref[...] / total_ref[...]
     joined = jnp.concatenate([attended[:, :rows], attended[:, rows:]], axis=0)
     rows = joined.T.astype(jnp.bfloat16).reshape(sources, 32, 128)
-    steps = out_ref.shape[0] // sources
-    rim = jnp.zeros((32, 128), jnp.bfloat16)
-    for step in range(steps):
-        start, stop = step * sources, (step + 1) * sources
-
-        @pl.when((pl.program_id(0) == step) & (parity_ref[0] == 0))
-        def _():
-            out_ref[start:stop, 0] = rows
-            if step == 0:
-                out_ref[0 : stop - 1, 1] = rows[1:]
-                out_ref[steps * sources - 1, 1] = rim
-            else:
-                out_ref[start - 1 : stop - 1, 1] = rows
-
-        @pl.when((pl.program_id(0) == step) & (parity_ref[0] == 1))
-        def _():
-            out_ref[start:stop, 1] = rows
-            if step == 0:
-                out_ref[0, 0] = rim
-            if step == steps - 1:
-                out_ref[start + 1 : stop, 0] = rows[:-1]
-            else:
-                out_ref[start + 1 : stop + 1, 0] = rows
-
-
-def attend(parity, own, other, sources=16, chunk=512):
+    rim = jnp.zeros((1, 32, 128), jnp.bfloat16)
+
+    @pl.when(parity_ref[0] == 0)
+    def _():
+        out_ref[:, 0] = rows
+        out_ref[:, 1] = jnp.concatenate([rows[1:], rim], axis=0)
+
+    @pl.when(parity_ref[0] == 1)
+    def _():
+        out_ref[:, 0] = jnp.concatenate([rim, rows[:-1]], axis=0)
+        out_ref[:, 1] = rows
+
+
+def attend(parity, own, other, chunk=512):
     count = own.shape[0]
     return pl.pallas_call(
-        functools.partial(attend_kernel, sources=sources, chunk=chunk),
-        grid=(count // sources,),
-        in_specs=[pl.BlockSpec(memory_space=pltpu.SMEM), whole(own.shape), whole(other.shape)],
-        out_specs=whole((count, 2, 32, 128)),
+        functools.partial(attend_kernel, chunk=chunk),
+        in_specs=[pl.BlockSpec(memory_space=pltpu.SMEM)] + [pl.BlockSpec(memory_space=pltpu.VMEM)] * 2,
         out_shape=jax.ShapeDtypeStruct((count, 2, 32, 128), jnp.bfloat16),
         scratch_shapes=[
             pltpu.VMEM((2 * count * 64, 128), jnp.bfloat16),
             pltpu.VMEM((64, 2 * count * 64), jnp.bfloat16),
-            pltpu.VMEM((8, 128), jnp.float32),
-            pltpu.VMEM((1, 64 * sources), jnp.float32),
-            pltpu.VMEM((64, 64 * sources), jnp.float32),
+            pltpu.VMEM((1, 64 * count), jnp.float32),
+            pltpu.VMEM((64, 64 * count), jnp.float32),
         ],
         compiler_params=pltpu.CompilerParams(vmem_limit_bytes=40 * MIB),
         name="attend",
@@ -418,6 +400,8 @@
     copies_ref,
     wide_two_ref,
     heat_ref,
+    held_ref,
+    final_held_ref,
     done,
 ):
     channels = bias_one_ref.shape[0]
@@ -430,16 +414,21 @@
         source = first_taps_ref.at[index] if index < 3 else last_taps_ref.at[0]
         slot = index % slots
         copies.append(pltpu.make_async_copy(source, weight_one_ref.at[slot], done.at[2 + index]))
+    near = pltpu.make_async_copy(resid_ref, held_ref, done.at[6])
+    final = pltpu.make_async_copy(final_ref, final_held_ref, done.at[7])
     first.start()
+    near.start()
     copies[0].start()
 
     attended = attended_rows(mixed_ref)
     first.wait()
+    near.wait()
     for copy in copies[1:]:
         copy.start()
     last.start()
+    final.start()
     projected = jnp.dot(attended, projection_ref[...], preferred_element_type=jnp.float32)
-    for place, resid in enumerate((above_ref[...], resid_ref[0], resid_ref[1], below_ref[...])):
+    for place, resid in enumerate((above_ref[...], held_ref[0], held_ref[1], below_ref[...])):
         rows = slice(64 * place, 64 * place + 64)
         stream = resid.astype(jnp.float32) + projected[rows]
         center = jnp.mean(stream, axis=-1, keepdims=True)
@@ -454,6 +443,7 @@
         copies[index].wait()
         if index == 3:
             last.wait()
+            final.wait()
         low = 64 if kernel_row < 2 else 0
         weight = weight_one_ref[index % slots].reshape(4 * channels, weight_one_ref.shape[3])
         product = dot_nt(field_ref[low : low + 192, :], weight)
@@ -491,7 +481,7 @@
                 store_strided(wide_two_ref, start, hidden[128 * place : 128 * place + 128])
     for row in range(8):
         hidden = load_wide(wide_two_ref, slice(256 * row, 256 * row + 256))
-        heat = dot_nt(final_ref[...], hidden) + final_bias_ref[...]
+        heat = dot_nt(final_held_ref[...], hidden) + final_bias_ref[...]
         heat_ref[row] = heat.astype(jnp.bfloat16)
     out_ref[...] = jnp.swapaxes(heat_ref[...], 0, 1)
 
@@ -520,8 +510,8 @@
     far = pl.BlockSpec(memory_space=pl.ANY)
     return pl.pallas_call(
         head_kernel,
-        in_specs=[pl.BlockSpec(memory_space=pltpu.SMEM), near, near, near, near, far, near, near]
-        + [far, far, near, far, near, near, near],
+        in_specs=[pl.BlockSpec(memory_space=pltpu.SMEM), near, far, near, near, far, near, near]
+        + [far, far, near, far, near, far, near],
         out_shape=jax.ShapeDtypeStruct((keypoints, 8, 256), jnp.bfloat16),
         scratch_shapes=[
             pltpu.VMEM(out_weight.shape, jnp.bfloat16),
@@ -533,7 +523,9 @@
             pltpu.VMEM((768, 3 * channels), jnp.bfloat16),
             pltpu.VMEM((channels // 128, 2048, 128), jnp.float32),
             pltpu.VMEM((8, keypoints, 256), jnp.bfloat16),
-            pltpu.SemaphoreType.DMA((6,)),
+            pltpu.VMEM(resid.shape, jnp.bfloat16),
+            pltpu.VMEM((keypoints, channels), jnp.bfloat16),
+            pltpu.SemaphoreType.DMA((8,)),
         ],
         compiler_params=pltpu.CompilerParams(vmem_limit_bytes=57 * MIB + MIB // 2),
         name="keypoint_head",

time: 92.1 us -> 88.5 us (0.961)
  Pallas kernels: 65 us -> 61.4 us
    pallas_call x1, Pallas kernels: 17.4 us -> 13.9 us  [attend(): pl.pallas_call(functools.partial(attend_kernel, chunk=chunk), in_specs=[p...]
  transfers between devices with their start and end apart: 5 -> 5, of which waited for: 3 -> 3; matrix products, arithmetic and copies ran while one was open for 1% -> 2% of each run, Pallas kernels for 28% -> 29%
where the time goes in v2:
time: 88.5 us; the launch traced here: 88 us
  Pallas kernels  61.4 us (69%)
  starting transfers between devices  16.3 us (18%)
  waiting for transfers between devices  7.78 us (9%)
  local copies, waits for them, and re-layouts  1.64 us (2%)
    pallas_call x2, Pallas kernels, reorder_taps(): pl.pallas_call(reorder_kernel, grid=(len(rows), channels // block), in_sp...  19.8 us
    pallas_call x1, Pallas kernels, keypoint_head(): pl.pallas_call(head_kernel, in_specs=[pl.BlockSpec(memory_space=pltpu.SME...  19.5 us
    pallas_call x1, Pallas kernels, attend(): pl.pallas_call(functools.partial(attend_kernel, chunk=chunk), in_specs=[p...  13.9 us
    all_to_all x1, starting transfers between devices, by_heads(): own = lax.all_to_all(packed, 'seq', 0, 0, tiled=True)  7.3 us
    pallas_call x1, Pallas kernels, pair_taps(): pl.pallas_call(pair_kernel, grid=(rows,), in_specs=[pl.BlockSpec((channel...  5.6 us
    all_to_all x1, starting transfers between devices, by_heads(): back = lax.all_to_all(sent, 'seq', 0, 0, tiled=True)  5.49 us
    all_to_all x1, waiting for transfers between devices, by_heads(): back = lax.all_to_all(sent, 'seq', 0, 0, tiled=True)  3.42 us
    pallas_call x1, Pallas kernels, pack_tokens(): pl.pallas_call(pack_kernel, in_specs=[pl.BlockSpec(memory_space=pl.ANY)]...  2.59 us
  transfers between devices with their start and end apart: 5, of which 3 were waited for; matrix products, arithmetic and copies ran while one was open for 2% of the time, Pallas kernels for 29%

profile of v2, /device:TPU:0, one launch (start us, length us, event | category | flops | bytes accessed | tf_op | source)
XLA Modules:
  0.0 88.0 jit_solution(18181478520368621307)
XLA Ops:
  0.0 2.6 %pack_tokens.1 = (bf16[32,96,128]{2,1,0:T(8,128)(2,1)}, bf16[64,1920]{1,0:T(8,128)(2,1)}, bf16[64,1920]{1,0:T(8,128)(2,1)}) custom-call(bf16[1,2,64,1024]{3,2,1,0:T(8,128)(2,1)} %query_ref.1, bf16[1,2,64,1024]{3,2,1,0:T(8,128)(2,1)} %keys_ref.1, bf16[1,2,64,1024]{3,2,1,0:T(8,128)(2,1)} %values_ref.1, bf16[1,2,64,1920]{3,2,1,0:T(8,128)(2,1)} %resid_ref.1), custom_call_target="tpu_custom_call" | custom-call | tf_op jit(solution)/shard_map/pack_tokens/pallas_call | solution.py:184
  2.6 7.3 %all-to-all-start = ((bf16[32,96,128]{2,1,0:T(8,128)(2,1)}), bf16[32,96,128]{2,1,0:T(8,128)(2,1)S(1)}, u32[]{:S(2)}, u32[]{:S(2)}) async-start(bf16[32,96,128]{2,1,0:T(8,128)(2,1)} %get-tuple-element.12.after_ref), calls=%async_computation | async-start | bytes 1572864 | tf_op jit(solution)/shard_map/all_to_all | solution.py:573
  9.9 2.2 %collective-permute-start = (bf16[64,1920]{1,0:T(8,128)(2,1)}, bf16[64,1920]{1,0:T(8,128)(2,1)S(1)}, u32[]{:S(2)}, u32[]{:S(2)}) collective-permute-start(bf16[64,1920]{1,0:T(8,128)(2,1)} %get-tuple-element.13), channel_id=1, source_target_pairs={{0,1},{1,2},{2,3},{3,4},{4,5},{5,6},{6,7},{7,8},{8,9},{9,10},{10,1... | collective-permute-start | bytes 737288 | tf_op jit(solution)/shard_map/ppermute | solution.py:574
  12.1 0.0 copy-start.3
  12.1 1.3 %collective-permute-start.1 = (bf16[64,1920]{1,0:T(8,128)(2,1)}, bf16[64,1920]{1,0:T(8,128)(2,1)S(1)}, u32[]{:S(2)}, u32[]{:S(2)}) collective-permute-start(bf16[64,1920]{1,0:T(8,128)(2,1)} %get-tuple-element.14), channel_id=1, source_target_pairs={{1,0},{2,1},{3,2},{4,3},{5,4},{6,5},{7,6},{8,7},{9,8},{10,9},{11,1... | collective-permute-start | bytes 737288 | tf_op jit(solution)/shard_map/ppermute | solution.py:575
  13.4 14.6 %reorder_taps.2.first_taps_ref = bf16[3,4,384,1920]{3,2,1,0:T(8,128)(2,1)} custom-call(bf16[384,4,4,1920]{3,2,1,0:T(4,128)(2,1)} %weight_ref.4, bf16[32,96,128]{2,1,0:T(8,128)(2,1)} %get-tuple-element.12.after_ref), custom_call_target="tpu_custom_call" | custom-call | bytes 35389440 | tf_op jit(solution)/shard_map/reorder_taps/pallas_call | solution.py:210
  28.0 0.0 collective-permute-done.above_ref
  28.1 0.0 copy-start.1
  28.1 0.0 collective-permute-done.1.below_ref
  28.1 0.0 copy-start.2
  28.1 2.5 %all-to-all-done.own_ref = bf16[32,96,128]{2,1,0:T(8,128)(2,1)S(1)} async-done(((bf16[32,96,128]{2,1,0:T(8,128)(2,1)}), bf16[32,96,128]{2,1,0:T(8,128)(2,1)S(1)}, u32[]{:S(2)}, u32[]{:S(2)}) %all-to-all-start) | async-done | bytes 786464 | tf_op jit(solution)/shard_map/all_to_all | solution.py:573
  30.5 0.1 slice.3
  30.6 0.1 collective-permute-start.2
  30.7 1.9 %collective-permute-done.2.other_ref = bf16[32,64,128]{2,1,0:T(8,128)(2,1)S(1)} collective-permute-done((bf16[32,64,128]{2,1,0:T(8,128)(2,1)S(1)}, bf16[32,64,128]{2,1,0:T(8,128)(2,1)S(1)}, u32[]{:S(2)}, u32[]{:S(2)}) %collective-permute-start.2) | collective-permute-done | bytes 524320 | tf_op jit(solution)/shard_map/ppermute | solution.py:578
  32.6 13.9 %attend.1.after_ref = bf16[32,2,32,128]{3,2,1,0:T(8,128)(2,1)} custom-call(s32[1]{0:T(128)} %bitcast.2.parity_ref, bf16[32,96,128]{2,1,0:T(8,128)(2,1)S(1)} %all-to-all-done.own_ref, bf16[32,64,128]{2,1,0:T(8,128)(2,1)S(1)} %collective-permute-done.2.other_ref), custom_call_target="tpu_custom_call" | custom-call | tf_op jit(solution)/shard_map/attend/pallas_call | solution.py:331
  46.4 5.5 %all-to-all-start.1 = ((bf16[32,2,32,128]{3,2,1,0:T(8,128)(2,1)}), bf16[32,2,32,128]{3,2,1,0:T(8,128)(2,1)S(1)}, u32[]{:S(2)}, u32[]{:S(2)}) async-start(bf16[32,2,32,128]{3,2,1,0:T(8,128)(2,1)} %attend.1.after_ref), calls=%async_computation.1 | async-start | bytes 1048576 | tf_op jit(solution)/shard_map/all_to_all | solution.py:582
  51.9 0.0 copy-done.3
  51.9 0.8 reshape.12.final_bias_ref
  52.7 0.6 add_convert_fusion.inside_ref
  53.3 5.1 %reorder_taps.3.last_taps_ref = bf16[1,4,384,1920]{3,2,1,0:T(8,128)(2,1)} custom-call(bf16[384,4,4,1920]{3,2,1,0:T(4,128)(2,1)} %weight_ref.4, bf16[32,2,32,128]{3,2,1,0:T(8,128)(2,1)} %attend.1.after_ref), custom_call_target="tpu_custom_call" | custom-call | bytes 11796480 | tf_op jit(solution)/shard_map/reorder_taps/pallas_call | solution.py:210
  58.4 0.0 copy-done.1
  58.4 0.0 copy-done.2
  58.4 5.6 %pair_taps.1.taps_two_ref = bf16[4,2,384,768]{3,2,1,0:T(8,128)(2,1)} custom-call(bf16[384,4,4,384]{3,2,1,0:T(4,128)(2,1)} %weight_ref.5, bf16[32,2,32,128]{3,2,1,0:T(8,128)(2,1)} %attend.1.after_ref), custom_call_target="tpu_custom_call" | custom-call | bytes 9437184 | tf_op jit(solution)/shard_map/pair_taps/pallas_call | solution.py:237
  64.0 3.4 %all-to-all-done.1 = bf16[32,2,32,128]{3,2,1,0:T(8,128)(2,1)S(1)} async-done(((bf16[32,2,32,128]{3,2,1,0:T(8,128)(2,1)}), bf16[32,2,32,128]{3,2,1,0:T(8,128)(2,1)S(1)}, u32[]{:S(2)}, u32[]{:S(2)}) %all-to-all-start.1) | async-done | bytes 524320 | tf_op jit(solution)/shard_map/all_to_all | solution.py:582
  67.5 0.0 copy-start
  67.5 0.8 copy-done
  68.3 19.5 %keypoint_head.1 = bf16[308,8,256]{2,1,0:T(8,128)(2,1)} custom-call(s32[2]{0:T(128)} %add_convert_fusion.inside_ref, bf16[16,2,2,32,128]{4,3,2,1,0:T(8,128)(2,1)} %bitcast.9, bf16[2,64,1920]{2,1,0:T(8,128)(2,1)} %bitcast.10, bf16[64,1920]{1,0:T(8,128)(2,1)} %copy-done.1, bf16[64,1920]{1,0:T(8,128)(2,1)} %copy-done.2, bf16[1024,1920]{1,0:T(8,128)(2,1)} %out_weight_ref.1, ...), custom_call_target="tpu_custom_call" | custom-call | tf_op jit(solution)/shard_map/keypoint_head/pallas_call | solution.py:511
Async XLA Ops:
  2.6 27.9 %all-to-all-start = ((bf16[32,96,128]{2,1,0:T(8,128)(2,1)}), bf16[32,96,128]{2,1,0:T(8,128)(2,1)S(1)}, u32[]{:S(2)}, u32[]{:S(2)}) async-start(bf16[32,96,128]{2,1,0:T(8,128)(2,1)} %get-tuple-element.12.after_ref), calls=%async_computation | async-start | bytes 1572864 | tf_op jit(solution)/shard_map/all_to_all | solution.py:573
  9.9 18.1 %collective-permute-start = (bf16[64,1920]{1,0:T(8,128)(2,1)}, bf16[64,1920]{1,0:T(8,128)(2,1)S(1)}, u32[]{:S(2)}, u32[]{:S(2)}) collective-permute-start(bf16[64,1920]{1,0:T(8,128)(2,1)} %get-tuple-element.13), channel_id=1, source_target_pairs={{0,1},{1,2},{2,3},{3,4},{4,5},{5,6},{6,7},{7,8},{8,9},{9,10},{10,1... | collective-permute-start | bytes 737288 | tf_op jit(solution)/shard_map/ppermute | solution.py:574
  12.1 39.8 %copy-start.3 = (f32[308]{0:T(512)S(1)}, f32[308]{0:T(512)}, u32[]{:S(2)}) copy-start(f32[308]{0:T(512)} %param.25) | copy-start | bytes 3700
  12.1 16.0 %collective-permute-start.1 = (bf16[64,1920]{1,0:T(8,128)(2,1)}, bf16[64,1920]{1,0:T(8,128)(2,1)S(1)}, u32[]{:S(2)}, u32[]{:S(2)}) collective-permute-start(bf16[64,1920]{1,0:T(8,128)(2,1)} %get-tuple-element.14), channel_id=1, source_target_pairs={{1,0},{2,1},{3,2},{4,3},{5,4},{6,5},{7,6},{8,7},{9,8},{10,9},{11,1... | collective-permute-start | bytes 737288 | tf_op jit(solution)/shard_map/ppermute | solution.py:575
  28.1 30.4 %copy-start.1 = (bf16[64,1920]{1,0:T(8,128)(2,1)}, bf16[64,1920]{1,0:T(8,128)(2,1)S(1)}, u32[]{:S(2)}) copy-start(bf16[64,1920]{1,0:T(8,128)(2,1)S(1)} %collective-permute-done.above_ref) | copy-start | bytes 737284
  28.1 30.4 %copy-start.2 = (bf16[64,1920]{1,0:T(8,128)(2,1)}, bf16[64,1920]{1,0:T(8,128)(2,1)S(1)}, u32[]{:S(2)}) copy-start(bf16[64,1920]{1,0:T(8,128)(2,1)S(1)} %collective-permute-done.1.below_ref) | copy-start | bytes 737284
  30.6 2.0 %collective-permute-start.2 = (bf16[32,64,128]{2,1,0:T(8,128)(2,1)S(1)}, bf16[32,64,128]{2,1,0:T(8,128)(2,1)S(1)}, u32[]{:S(2)}, u32[]{:S(2)}) collective-permute-start(bf16[32,64,128]{2,1,0:T(8,128)(2,1)S(1)} %slice.3), channel_id=1, source_target_pairs={{0,1},{1,0},{2,3},{3,2},{4,5},{5,4},{6,7},{7,6},{8,9},{9,8},{10,11... | collective-permute-start | bytes 1572872 | tf_op jit(solution)/shard_map/ppermute | solution.py:578
  46.4 21.0 %all-to-all-start.1 = ((bf16[32,2,32,128]{3,2,1,0:T(8,128)(2,1)}), bf16[32,2,32,128]{3,2,1,0:T(8,128)(2,1)S(1)}, u32[]{:S(2)}, u32[]{:S(2)}) async-start(bf16[32,2,32,128]{3,2,1,0:T(8,128)(2,1)} %attend.1.after_ref), calls=%async_computation.1 | async-start | bytes 1048576 | tf_op jit(solution)/shard_map/all_to_all | solution.py:582
  67.5 0.8 copy-start

commit v3 on v2

--- a/solution.py
+++ b/solution.py
@@ -401,7 +401,6 @@
     wide_two_ref,
     heat_ref,
     held_ref,
-    final_held_ref,
     done,
 ):
     channels = bias_one_ref.shape[0]
@@ -415,7 +414,6 @@
         slot = index % slots
         copies.append(pltpu.make_async_copy(source, weight_one_ref.at[slot], done.at[2 + index]))
     near = pltpu.make_async_copy(resid_ref, held_ref, done.at[6])
-    final = pltpu.make_async_copy(final_ref, final_held_ref, done.at[7])
     first.start()
     near.start()
     copies[0].start()
@@ -426,7 +424,6 @@
     for copy in copies[1:]:
         copy.start()
     last.start()
-    final.start()
     projected = jnp.dot(attended, projection_ref[...], preferred_element_type=jnp.float32)
     for place, resid in enumerate((above_ref[...], held_ref[0], held_ref[1], below_ref[...])):
         rows = slice(64 * place, 64 * place + 64)
@@ -443,7 +440,6 @@
         copies[index].wait()
         if index == 3:
             last.wait()
-            final.wait()
         low = 64 if kernel_row < 2 else 0
         weight = weight_one_ref[index % slots].reshape(4 * channels, weight_one_ref.shape[3])
         product = dot_nt(field_ref[low : low + 192, :], weight)
@@ -481,7 +477,7 @@
                 store_strided(wide_two_ref, start, hidden[128 * place : 128 * place + 128])
     for row in range(8):
         hidden = load_wide(wide_two_ref, slice(256 * row, 256 * row + 256))
-        heat = dot_nt(final_held_ref[...], hidden) + final_bias_ref[...]
+        heat = dot_nt(final_ref[...], hidden) + final_bias_ref[...]
         heat_ref[row] = heat.astype(jnp.bfloat16)
     out_ref[...] = jnp.swapaxes(heat_ref[...], 0, 1)
 
@@ -511,7 +507,7 @@
     return pl.pallas_call(
         head_kernel,
         in_specs=[pl.BlockSpec(memory_space=pltpu.SMEM), near, far, near, near, far, near, near]
-        + [far, far, near, far, near, far, near],
+        + [far, far, near, far, near, near, near],
         out_shape=jax.ShapeDtypeStruct((keypoints, 8, 256), jnp.bfloat16),
         scratch_shapes=[
             pltpu.VMEM(out_weight.shape, jnp.bfloat16),
@@ -524,8 +520,7 @@
             pltpu.VMEM((channels // 128, 2048, 128), jnp.float32),
             pltpu.VMEM((8, keypoints, 256), jnp.bfloat16),
             pltpu.VMEM(resid.shape, jnp.bfloat16),
-            pltpu.VMEM((keypoints, channels), jnp.bfloat16),
-            pltpu.SemaphoreType.DMA((8,)),
+            pltpu.SemaphoreType.DMA((7,)),
         ],
         compiler_params=pltpu.CompilerParams(vmem_limit_bytes=57 * MIB + MIB // 2),
         name="keypoint_head",

time: 88.5 us -> 88.6 us (level)
  no operation moved by 1% of the time
where the time goes in v3:
time: 88.6 us; the launch traced here: 88.1 us
  Pallas kernels  61.5 us (69%)
  starting transfers between devices  16.3 us (18%)
  waiting for transfers between devices  7.78 us (9%)
  local copies, waits for them, and re-layouts  1.64 us (2%)
    pallas_call x2, Pallas kernels, reorder_taps(): pl.pallas_call(reorder_kernel, grid=(len(rows), channels // block), in_sp...  19.8 us
    pallas_call x1, Pallas kernels, keypoint_head(): pl.pallas_call(head_kernel, in_specs=[pl.BlockSpec(memory_space=pltpu.SME...  19.6 us
    pallas_call x1, Pallas kernels, attend(): pl.pallas_call(functools.partial(attend_kernel, chunk=chunk), in_specs=[p...  13.9 us
    all_to_all x1, starting transfers between devices, by_heads(): own = lax.all_to_all(packed, 'seq', 0, 0, tiled=True)  7.3 us
    pallas_call x1, Pallas kernels, pair_taps(): pl.pallas_call(pair_kernel, grid=(rows,), in_specs=[pl.BlockSpec((channel...  5.6 us
    all_to_all x1, starting transfers between devices, by_heads(): back = lax.all_to_all(sent, 'seq', 0, 0, tiled=True)  5.49 us
    all_to_all x1, waiting for transfers between devices, by_heads(): back = lax.all_to_all(sent, 'seq', 0, 0, tiled=True)  3.42 us
    pallas_call x1, Pallas kernels, pack_tokens(): pl.pallas_call(pack_kernel, in_specs=[pl.BlockSpec(memory_space=pl.ANY)]...  2.59 us
  transfers between devices with their start and end apart: 5, of which 3 were waited for; matrix products, arithmetic and copies ran while one was open for 2% of the time, Pallas kernels for 29%

profile of v3, /device:TPU:0, one launch (start us, length us, event | category | flops | bytes accessed | tf_op | source)
XLA Modules:
  0.0 88.1 jit_solution(11482870282475931520)
XLA Ops:
  0.0 2.6 %pack_tokens.1 = (bf16[32,96,128]{2,1,0:T(8,128)(2,1)}, bf16[64,1920]{1,0:T(8,128)(2,1)}, bf16[64,1920]{1,0:T(8,128)(2,1)}) custom-call(bf16[1,2,64,1024]{3,2,1,0:T(8,128)(2,1)} %query_ref.1, bf16[1,2,64,1024]{3,2,1,0:T(8,128)(2,1)} %keys_ref.1, bf16[1,2,64,1024]{3,2,1,0:T(8,128)(2,1)} %values_ref.1, bf16[1,2,64,1920]{3,2,1,0:T(8,128)(2,1)} %resid_ref.1), custom_call_target="tpu_custom_call" | custom-call | tf_op jit(solution)/shard_map/pack_tokens/pallas_call | solution.py:184
  2.6 7.3 %all-to-all-start = ((bf16[32,96,128]{2,1,0:T(8,128)(2,1)}), bf16[32,96,128]{2,1,0:T(8,128)(2,1)S(1)}, u32[]{:S(2)}, u32[]{:S(2)}) async-start(bf16[32,96,128]{2,1,0:T(8,128)(2,1)} %get-tuple-element.12.after_ref), calls=%async_computation | async-start | bytes 1572864 | tf_op jit(solution)/shard_map/all_to_all | solution.py:568
  9.9 2.2 %collective-permute-start = (bf16[64,1920]{1,0:T(8,128)(2,1)}, bf16[64,1920]{1,0:T(8,128)(2,1)S(1)}, u32[]{:S(2)}, u32[]{:S(2)}) collective-permute-start(bf16[64,1920]{1,0:T(8,128)(2,1)} %get-tuple-element.13), channel_id=1, source_target_pairs={{0,1},{1,2},{2,3},{3,4},{4,5},{5,6},{6,7},{7,8},{8,9},{9,10},{10,1... | collective-permute-start | bytes 737288 | tf_op jit(solution)/shard_map/ppermute | solution.py:569
  12.1 0.0 copy-start.3
  12.1 1.3 %collective-permute-start.1 = (bf16[64,1920]{1,0:T(8,128)(2,1)}, bf16[64,1920]{1,0:T(8,128)(2,1)S(1)}, u32[]{:S(2)}, u32[]{:S(2)}) collective-permute-start(bf16[64,1920]{1,0:T(8,128)(2,1)} %get-tuple-element.14), channel_id=1, source_target_pairs={{1,0},{2,1},{3,2},{4,3},{5,4},{6,5},{7,6},{8,7},{9,8},{10,9},{11,1... | collective-permute-start | bytes 737288 | tf_op jit(solution)/shard_map/ppermute | solution.py:570
  13.4 14.6 %reorder_taps.2.first_taps_ref = bf16[3,4,384,1920]{3,2,1,0:T(8,128)(2,1)} custom-call(bf16[384,4,4,1920]{3,2,1,0:T(4,128)(2,1)} %weight_ref.4, bf16[32,96,128]{2,1,0:T(8,128)(2,1)} %get-tuple-element.12.after_ref), custom_call_target="tpu_custom_call" | custom-call | bytes 35389440 | tf_op jit(solution)/shard_map/reorder_taps/pallas_call | solution.py:210
  28.0 0.0 collective-permute-done.above_ref
  28.1 0.0 copy-start.1
  28.1 0.0 collective-permute-done.1.below_ref
  28.1 0.0 copy-start.2
  28.1 2.5 %all-to-all-done.own_ref = bf16[32,96,128]{2,1,0:T(8,128)(2,1)S(1)} async-done(((bf16[32,96,128]{2,1,0:T(8,128)(2,1)}), bf16[32,96,128]{2,1,0:T(8,128)(2,1)S(1)}, u32[]{:S(2)}, u32[]{:S(2)}) %all-to-all-start) | async-done | bytes 786464 | tf_op jit(solution)/shard_map/all_to_all | solution.py:568
  30.5 0.1 slice.3
  30.6 0.1 collective-permute-start.2
  30.7 1.9 %collective-permute-done.2.other_ref = bf16[32,64,128]{2,1,0:T(8,128)(2,1)S(1)} collective-permute-done((bf16[32,64,128]{2,1,0:T(8,128)(2,1)S(1)}, bf16[32,64,128]{2,1,0:T(8,128)(2,1)S(1)}, u32[]{:S(2)}, u32[]{:S(2)}) %collective-permute-start.2) | collective-permute-done | bytes 524320 | tf_op jit(solution)/shard_map/ppermute | solution.py:573
  32.6 13.9 %attend.1.after_ref = bf16[32,2,32,128]{3,2,1,0:T(8,128)(2,1)} custom-call(s32[1]{0:T(128)} %bitcast.2.parity_ref, bf16[32,96,128]{2,1,0:T(8,128)(2,1)S(1)} %all-to-all-done.own_ref, bf16[32,64,128]{2,1,0:T(8,128)(2,1)S(1)} %collective-permute-done.2.other_ref), custom_call_target="tpu_custom_call" | custom-call | tf_op jit(solution)/shard_map/attend/pallas_call | solution.py:331
  46.4 5.5 %all-to-all-start.1 = ((bf16[32,2,32,128]{3,2,1,0:T(8,128)(2,1)}), bf16[32,2,32,128]{3,2,1,0:T(8,128)(2,1)S(1)}, u32[]{:S(2)}, u32[]{:S(2)}) async-start(bf16[32,2,32,128]{3,2,1,0:T(8,128)(2,1)} %attend.1.after_ref), calls=%async_computation.1 | async-start | bytes 1048576 | tf_op jit(solution)/shard_map/all_to_all | solution.py:577
  51.9 0.0 copy-done.3
  51.9 0.8 reshape.12.final_bias_ref
  52.7 0.6 add_convert_fusion.inside_ref
  53.3 5.1 %reorder_taps.3.last_taps_ref = bf16[1,4,384,1920]{3,2,1,0:T(8,128)(2,1)} custom-call(bf16[384,4,4,1920]{3,2,1,0:T(4,128)(2,1)} %weight_ref.4, bf16[32,2,32,128]{3,2,1,0:T(8,128)(2,1)} %attend.1.after_ref), custom_call_target="tpu_custom_call" | custom-call | bytes 11796480 | tf_op jit(solution)/shard_map/reorder_taps/pallas_call | solution.py:210
  58.4 0.0 copy-done.1
  58.4 0.0 copy-done.2
  58.4 5.6 %pair_taps.1.taps_two_ref = bf16[4,2,384,768]{3,2,1,0:T(8,128)(2,1)} custom-call(bf16[384,4,4,384]{3,2,1,0:T(4,128)(2,1)} %weight_ref.5, bf16[32,2,32,128]{3,2,1,0:T(8,128)(2,1)} %attend.1.after_ref), custom_call_target="tpu_custom_call" | custom-call | bytes 9437184 | tf_op jit(solution)/shard_map/pair_taps/pallas_call | solution.py:237
  64.0 3.4 %all-to-all-done.1 = bf16[32,2,32,128]{3,2,1,0:T(8,128)(2,1)S(1)} async-done(((bf16[32,2,32,128]{3,2,1,0:T(8,128)(2,1)}), bf16[32,2,32,128]{3,2,1,0:T(8,128)(2,1)S(1)}, u32[]{:S(2)}, u32[]{:S(2)}) %all-to-all-start.1) | async-done | bytes 524320 | tf_op jit(solution)/shard_map/all_to_all | solution.py:577
  67.5 0.0 copy-start
  67.5 0.8 copy-done
  68.3 19.6 %keypoint_head.1 = bf16[308,8,256]{2,1,0:T(8,128)(2,1)} custom-call(s32[2]{0:T(128)} %add_convert_fusion.inside_ref, bf16[16,2,2,32,128]{4,3,2,1,0:T(8,128)(2,1)} %bitcast.9, bf16[2,64,1920]{2,1,0:T(8,128)(2,1)} %bitcast.10, bf16[64,1920]{1,0:T(8,128)(2,1)} %copy-done.1, bf16[64,1920]{1,0:T(8,128)(2,1)} %copy-done.2, bf16[1024,1920]{1,0:T(8,128)(2,1)} %out_weight_ref.1, ...), custom_call_target="tpu_custom_call" | custom-call | tf_op jit(solution)/shard_map/keypoint_head/pallas_call | solution.py:507
Async XLA Ops:
  2.6 27.9 %all-to-all-start = ((bf16[32,96,128]{2,1,0:T(8,128)(2,1)}), bf16[32,96,128]{2,1,0:T(8,128)(2,1)S(1)}, u32[]{:S(2)}, u32[]{:S(2)}) async-start(bf16[32,96,128]{2,1,0:T(8,128)(2,1)} %get-tuple-element.12.after_ref), calls=%async_computation | async-start | bytes 1572864 | tf_op jit(solution)/shard_map/all_to_all | solution.py:568
  9.9 18.1 %collective-permute-start = (bf16[64,1920]{1,0:T(8,128)(2,1)}, bf16[64,1920]{1,0:T(8,128)(2,1)S(1)}, u32[]{:S(2)}, u32[]{:S(2)}) collective-permute-start(bf16[64,1920]{1,0:T(8,128)(2,1)} %get-tuple-element.13), channel_id=1, source_target_pairs={{0,1},{1,2},{2,3},{3,4},{4,5},{5,6},{6,7},{7,8},{8,9},{9,10},{10,1... | collective-permute-start | bytes 737288 | tf_op jit(solution)/shard_map/ppermute | solution.py:569
  12.1 39.8 %copy-start.3 = (f32[308]{0:T(512)S(1)}, f32[308]{0:T(512)}, u32[]{:S(2)}) copy-start(f32[308]{0:T(512)} %param.25) | copy-start | bytes 3700
  12.1 16.0 %collective-permute-start.1 = (bf16[64,1920]{1,0:T(8,128)(2,1)}, bf16[64,1920]{1,0:T(8,128)(2,1)S(1)}, u32[]{:S(2)}, u32[]{:S(2)}) collective-permute-start(bf16[64,1920]{1,0:T(8,128)(2,1)} %get-tuple-element.14), channel_id=1, source_target_pairs={{1,0},{2,1},{3,2},{4,3},{5,4},{6,5},{7,6},{8,7},{9,8},{10,9},{11,1... | collective-permute-start | bytes 737288 | tf_op jit(solution)/shard_map/ppermute | solution.py:570
  28.1 30.4 %copy-start.1 = (bf16[64,1920]{1,0:T(8,128)(2,1)}, bf16[64,1920]{1,0:T(8,128)(2,1)S(1)}, u32[]{:S(2)}) copy-start(bf16[64,1920]{1,0:T(8,128)(2,1)S(1)} %collective-permute-done.above_ref) | copy-start | bytes 737284
  28.1 30.4 %copy-start.2 = (bf16[64,1920]{1,0:T(8,128)(2,1)}, bf16[64,1920]{1,0:T(8,128)(2,1)S(1)}, u32[]{:S(2)}) copy-start(bf16[64,1920]{1,0:T(8,128)(2,1)S(1)} %collective-permute-done.1.below_ref) | copy-start | bytes 737284
  30.6 2.0 %collective-permute-start.2 = (bf16[32,64,128]{2,1,0:T(8,128)(2,1)S(1)}, bf16[32,64,128]{2,1,0:T(8,128)(2,1)S(1)}, u32[]{:S(2)}, u32[]{:S(2)}) collective-permute-start(bf16[32,64,128]{2,1,0:T(8,128)(2,1)S(1)} %slice.3), channel_id=1, source_target_pairs={{0,1},{1,0},{2,3},{3,2},{4,5},{5,4},{6,7},{7,6},{8,9},{9,8},{10,11... | collective-permute-start | bytes 1572872 | tf_op jit(solution)/shard_map/ppermute | solution.py:573
  46.4 21.0 %all-to-all-start.1 = ((bf16[32,2,32,128]{3,2,1,0:T(8,128)(2,1)}), bf16[32,2,32,128]{3,2,1,0:T(8,128)(2,1)S(1)}, u32[]{:S(2)}, u32[]{:S(2)}) async-start(bf16[32,2,32,128]{3,2,1,0:T(8,128)(2,1)} %attend.1.after_ref), calls=%async_computation.1 | async-start | bytes 1048576 | tf_op jit(solution)/shard_map/all_to_all | solution.py:577
  67.5 0.8 copy-start
